TPU v7x, 128 devices: a whole 4x4x4 slice. The times are simulated.
128 devices in a mesh: seq: 2 (over x_lo), ctx: 32 (over y, z, core), tp: 2 (over x_hi).
Axes of the slice: x: 4 (x_hi: 2, x_lo: 2; x = x_hi * 2 + x_lo), y: 4, z: 4, core: 2. Of those that a mesh axis runs over, the one named last changes fastest.
Arguments:
- inputs: bfloat16 [2, 8192, 896], P('seq', 'ctx'), may hold values from -6 to 6
- positions: int32 [2, 8192], P('seq', 'ctx'), may hold values from 0 to 8063, as said below
- query_key_value_weight: bfloat16 [896, 2, 576], P(('seq', 'ctx'), 'tp'), may hold values from -0.1875 to 0.1875
- query_key_value_bias: bfloat16 [2, 576], P('tp', ('seq', 'ctx')), may hold values from -3 to 3
- gain_attn: bfloat16 [896], P(('seq', 'ctx')), may hold values from 0.099609375 to 1.8984375
- output_weight: bfloat16 [2, 448, 896], P('tp', None, ('seq', 'ctx')), may hold values from -6 to 6
- gate_weight: bfloat16 [896, 4864], P(('seq', 'ctx'), 'tp'), may hold values from -0.1875 to 0.1875
- up_weight: bfloat16 [896, 4864], P(('seq', 'ctx'), 'tp'), may hold values from -0.1875 to 0.1875
- down_weight: bfloat16 [4864, 896], P('tp', ('seq', 'ctx')), may hold values from -0.078125 to 0.078125
- gain_ffn: bfloat16 [896], P(('seq', 'ctx')), may hold values from 0.099609375 to 1.8984375
- cotangent: bfloat16 [2, 8192, 896], P('seq', 'ctx'), may hold values from -6 to 6
Outputs:
- output: bfloat16 [2, 8192, 896], P('seq', 'ctx')
- grad_inputs: bfloat16 [2, 8192, 896], P('seq', 'ctx')
- grad_w_qkv: float32 [896, 2, 576], P(('seq', 'ctx'), 'tp')
- grad_b_qk: float32 [2, 512], P('tp', ('seq', 'ctx'))
- grad_b_v: float32 [2, 64], P('tp', ('seq', 'ctx'))
- grad_gain_attn: float32 [896], P(('seq', 'ctx'))
- grad_w_out: float32 [2, 448, 896], P('tp', None, ('seq', 'ctx'))
- grad_w_gate: float32 [896, 4864], P(('seq', 'ctx'), 'tp')
- grad_w_up: float32 [896, 4864], P(('seq', 'ctx'), 'tp')
- grad_w_down: float32 [4864, 896], P('tp', ('seq', 'ctx'))
- grad_gain_ffn: float32 [896], P(('seq', 'ctx'))
Inputs may be any that keep to these rules, and one draw needn't show every extreme that they name: Each sequence is a pack of three documents: positions count 0, 1, 2, ... along a document and restart at 0 at its first token; the first document ends within the sequence's first 128 tokens, the third begins at token 128 and runs to the sequence's end.
All inputs are finite; a program needn't handle non-finite values.
Results may differ from a plain program's by a relative error of at most 0.035.
Values may be sent and summed in bfloat16 or wider, within the bound.
A program may use at most 128 MiB of HBM per device.

v0:
```python
import math

import jax
import jax.numpy as jnp
from jax import lax
from jax.sharding import PartitionSpec as P

HEADS = 14
KVH = 2
HD = 64


EPS_VALUE = 1e-06
THETA = 1000000.0
NEGATIVE = -1e30
KEY_BLOCK = 512


def rope_tables(positions):
    exponents = jnp.arange(HD // 2, dtype=jnp.float32) * (2.0 / HD)
    freqs = THETA ** (-exponents)
    angles = positions.astype(jnp.float32)[..., None] * freqs
    angles = jnp.concatenate([angles, angles], -1)
    return (jnp.cos(angles), jnp.sin(angles))


def rotate(values, cosine, sine_table):
    half_width = values.shape[-1] // 2
    turned = jnp.concatenate([-values[..., half_width:], values[..., :half_width]], -1)
    return values * cosine + turned * sine_table


def rotate_back(grads, cosine, sine_table):
    half_width = grads.shape[-1] // 2
    sined = grads * sine_table
    return grads * cosine + jnp.concatenate([sined[..., half_width:], -sined[..., :half_width]], -1)


def norm_back(values, inv_rms, gain, grad_normed):
    scaled = grad_normed * gain
    grad_gain = jnp.sum(grad_normed * values * inv_rms, 0)
    grad_values = inv_rms * scaled - values * inv_rms**3 * jnp.mean(
        scaled * values, -1, keepdims=True
    )
    return (grad_gain, grad_values)


def key_blocks(shard_rows, running, block_fn, last_query, first_start):
    row_count = shard_rows.shape[0]
    key_count = math.gcd(row_count, KEY_BLOCK)
    pieces = shard_rows.reshape(row_count // key_count, key_count, shard_rows.shape[1])
    offsets = jnp.arange(row_count // key_count, dtype=jnp.int32) * key_count

    def scan_body(state, items):
        piece, offset = items
        needed = (offset <= last_query) & (offset + key_count > first_start)
        state = lax.cond(
            needed, lambda inner: block_fn(inner, piece, offset), lambda inner: inner, state
        )
        return (state, None)

    running, unused = lax.scan(scan_body, running, (pieces, offsets))
    return running


def unit_sum(partial_sum):
    return lax.psum(partial_sum.astype(jnp.bfloat16), "tp").astype(jnp.float32)


def shards(
    inputs,
    positions,
    query_key_value_weight,
    query_key_value_bias,
    gain_attn,
    output_weight,
    gate_weight,
    up_weight,
    down_weight,
    gain_ffn,
    cotangent,
):
    tokens_here = inputs.shape[1]
    ctx_count = lax.axis_size("ctx")
    heads_here = HEADS // KVH
    group_q = heads_here * HD
    scale = HD ** (-0.5)
    row_index = lax.axis_index("ctx") * tokens_here + jnp.arange(tokens_here, dtype=jnp.int32)
    position_row = positions[0]
    doc_start = row_index - position_row
    last_query = row_index[-1]
    first_start = jnp.min(doc_start)
    cosine, sine_table = rope_tables(position_row)
    inputs_f = inputs[0].astype(jnp.float32)
    qkv_full, bias_full, gain_one, out_full = (
        lax.all_gather(query_key_value_weight, ("seq", "ctx"), axis=0, tiled=True),
        lax.all_gather(query_key_value_bias, ("seq", "ctx"), axis=1, tiled=True),
        lax.all_gather(gain_attn, ("seq", "ctx"), axis=0, tiled=True),
        lax.all_gather(output_weight, ("seq", "ctx"), axis=2, tiled=True),
    )
    gate_full, up_full, down_full, gain_two = (
        lax.all_gather(gate_weight, ("seq", "ctx"), axis=0, tiled=True),
        lax.all_gather(up_weight, ("seq", "ctx"), axis=0, tiled=True),
        lax.all_gather(down_weight, ("seq", "ctx"), axis=1, tiled=True),
        lax.all_gather(gain_ffn, ("seq", "ctx"), axis=0, tiled=True),
    )
    inv_first = lax.rsqrt(jnp.mean(inputs_f * inputs_f, -1, keepdims=True) + EPS_VALUE)
    normalized_input = (inputs_f * inv_first * gain_one.astype(jnp.float32)).astype(jnp.bfloat16)
    projected_attention = jnp.dot(
        normalized_input, qkv_full[:, 0, :], preferred_element_type=jnp.float32
    ) + bias_full[0].astype(jnp.float32)
    queries = rotate(
        projected_attention[:, :group_q].reshape(tokens_here, heads_here, HD),
        cosine[:, None, :],
        sine_table[:, None, :],
    ).astype(jnp.bfloat16)
    key_rows = rotate(projected_attention[:, group_q : group_q + HD], cosine, sine_table).astype(
        jnp.bfloat16
    )
    value_rows = projected_attention[:, group_q + HD :].astype(jnp.bfloat16)
    key_values = jnp.concatenate([key_rows, value_rows], -1)

    def masked_scores(key_block, offset):
        key_count = key_block.shape[0]
        scores = (
            jnp.einsum(
                "thd,sd->hts", queries, key_block[:, :HD], preferred_element_type=jnp.float32
            )
            * scale
        )
        key_index = offset + jnp.arange(key_count, dtype=jnp.int32)
        visible = (key_index[None, :] >= doc_start[:, None]) & (
            key_index[None, :] <= row_index[:, None]
        )
        return (jnp.where(visible[None], scores, NEGATIVE), visible)

    def forward_block(running, key_block, offset):
        row_max, row_total, weighted = running
        scores, visible = masked_scores(key_block, offset)
        new_max = jnp.maximum(row_max, jnp.max(scores, -1))
        rescale = jnp.exp(row_max - new_max)
        attn_probs = jnp.where(visible[None], jnp.exp(scores - new_max[..., None]), 0.0)
        row_total = row_total * rescale + jnp.sum(attn_probs, -1)
        weighted = weighted * rescale[..., None] + jnp.einsum(
            "hts,sd->htd",
            attn_probs.astype(jnp.bfloat16),
            key_block[:, HD:],
            preferred_element_type=jnp.float32,
        )
        return (new_max, row_total, weighted)

    initial = (
        jnp.full((heads_here, tokens_here), NEGATIVE, jnp.float32),
        jnp.zeros((heads_here, tokens_here), jnp.float32),
        jnp.zeros((heads_here, tokens_here, HD), jnp.float32),
    )
    row_max, row_total, weighted = key_blocks(
        lax.all_gather(key_values, "ctx", axis=0, tiled=True),
        initial,
        forward_block,
        last_query,
        first_start,
    )
    attention_output = weighted / row_total[..., None]
    log_total = row_max + jnp.log(row_total)
    attended_low = (
        attention_output.transpose(1, 0, 2).reshape(tokens_here, group_q).astype(jnp.bfloat16)
    )
    residual_branch = unit_sum(
        jnp.dot(attended_low, out_full[0], preferred_element_type=jnp.float32)
    )
    middle_state = inputs_f + residual_branch
    inv_second = lax.rsqrt(jnp.mean(middle_state * middle_state, -1, keepdims=True) + EPS_VALUE)
    normalized_feedforward_input = (
        middle_state * inv_second * gain_two.astype(jnp.float32)
    ).astype(jnp.bfloat16)
    gate_activation = jnp.dot(
        normalized_feedforward_input, gate_full, preferred_element_type=jnp.float32
    )
    up_activation = jnp.dot(
        normalized_feedforward_input, up_full, preferred_element_type=jnp.float32
    )
    hidden_state = (jax.nn.silu(gate_activation) * up_activation).astype(jnp.bfloat16)
    output = middle_state + unit_sum(
        jnp.dot(hidden_state, down_full, preferred_element_type=jnp.float32)
    )
    gate_back, up_back, down_back, gain_two_back = (
        lax.all_gather(gate_weight, ("seq", "ctx"), axis=0, tiled=True),
        lax.all_gather(up_weight, ("seq", "ctx"), axis=0, tiled=True),
        lax.all_gather(down_weight, ("seq", "ctx"), axis=1, tiled=True),
        lax.all_gather(gain_ffn, ("seq", "ctx"), axis=0, tiled=True),
    )
    qkv_back, bias_unused, gain_one_back, out_back = (
        lax.all_gather(query_key_value_weight, ("seq", "ctx"), axis=0, tiled=True),
        lax.all_gather(query_key_value_bias, ("seq", "ctx"), axis=1, tiled=True),
        lax.all_gather(gain_attn, ("seq", "ctx"), axis=0, tiled=True),
        lax.all_gather(output_weight, ("seq", "ctx"), axis=2, tiled=True),
    )
    grad_out_low = cotangent[0]
    grad_out = grad_out_low.astype(jnp.float32)
    grad_down = jnp.einsum(
        "tf,td->fd", hidden_state, grad_out_low, preferred_element_type=jnp.float32
    )
    grad_hidden = jnp.einsum(
        "td,fd->tf", grad_out_low, down_back, preferred_element_type=jnp.float32
    )
    sigmoid_gate = jax.nn.sigmoid(gate_activation)
    grad_up_act = (grad_hidden * (gate_activation * sigmoid_gate)).astype(jnp.bfloat16)
    grad_gate_act = (
        grad_hidden * up_activation * sigmoid_gate * (1.0 + gate_activation * (1.0 - sigmoid_gate))
    ).astype(jnp.bfloat16)
    grad_gate_w = jnp.einsum(
        "td,tf->df", normalized_feedforward_input, grad_gate_act, preferred_element_type=jnp.float32
    )
    grad_up_w = jnp.einsum(
        "td,tf->df", normalized_feedforward_input, grad_up_act, preferred_element_type=jnp.float32
    )
    grad_normed_ffn = unit_sum(
        jnp.einsum("tf,df->td", grad_gate_act, gate_back, preferred_element_type=jnp.float32)
        + jnp.einsum("tf,df->td", grad_up_act, up_back, preferred_element_type=jnp.float32)
    )
    grad_gain_two, grad_middle_norm = norm_back(
        middle_state, inv_second, gain_two_back.astype(jnp.float32), grad_normed_ffn
    )
    grad_middle = grad_out + grad_middle_norm
    grad_branch = grad_middle.astype(jnp.bfloat16)
    grad_out_w = jnp.einsum(
        "tc,td->cd", attended_low, grad_branch, preferred_element_type=jnp.float32
    )
    grad_attended = jnp.einsum(
        "td,cd->tc", grad_branch, out_back[0], preferred_element_type=jnp.float32
    ).astype(jnp.bfloat16)
    grad_attended = grad_attended.reshape(tokens_here, heads_here, HD).transpose(1, 0, 2)
    row_delta = jnp.sum(grad_attended.astype(jnp.float32) * attention_output, -1)

    def backward_block(running, key_block, offset):
        grad_query, grad_kv = running
        key_count = key_block.shape[0]
        scores, visible = masked_scores(key_block, offset)
        attn_probs = jnp.where(visible[None], jnp.exp(scores - log_total[..., None]), 0.0)
        grad_probs = jnp.einsum(
            "htd,sd->hts", grad_attended, key_block[:, HD:], preferred_element_type=jnp.float32
        )
        grad_scores = (attn_probs * (grad_probs - row_delta[..., None])).astype(jnp.bfloat16)
        grad_query = grad_query + scale * jnp.einsum(
            "hts,sd->htd", grad_scores, key_block[:, :HD], preferred_element_type=jnp.float32
        )
        grad_keys = scale * jnp.einsum(
            "hts,thd->sd", grad_scores, queries, preferred_element_type=jnp.float32
        )
        grad_values = jnp.einsum(
            "hts,htd->sd",
            attn_probs.astype(jnp.bfloat16),
            grad_attended,
            preferred_element_type=jnp.float32,
        )
        current = lax.dynamic_slice_in_dim(grad_kv, offset, key_count, 0)
        grad_kv = lax.dynamic_update_slice_in_dim(
            grad_kv, current + jnp.concatenate([grad_keys, grad_values], -1), offset, 0
        )
        return (grad_query, grad_kv)

    start_back = (
        jnp.zeros((heads_here, tokens_here, HD), jnp.float32),
        jnp.zeros((tokens_here * ctx_count, 2 * HD), jnp.float32),
    )
    grad_query, grad_kv = key_blocks(
        lax.all_gather(key_values, "ctx", axis=0, tiled=True),
        start_back,
        backward_block,
        last_query,
        first_start,
    )
    grad_kv_mine = lax.psum_scatter(
        grad_kv.astype(jnp.bfloat16), "ctx", scatter_dimension=0, tiled=True
    ).astype(jnp.float32)
    grad_q_lin = rotate_back(
        grad_query.transpose(1, 0, 2), cosine[:, None, :], sine_table[:, None, :]
    ).reshape(tokens_here, group_q)
    grad_k_lin = rotate_back(grad_kv_mine[:, :HD], cosine, sine_table)
    grad_mixed = jnp.concatenate([grad_q_lin, grad_k_lin, grad_kv_mine[:, HD:]], -1).astype(
        jnp.bfloat16
    )
    grad_bias = jnp.sum(grad_mixed.astype(jnp.float32), 0)
    split_at = group_q + HD
    grad_qkv_w = jnp.einsum(
        "td,tc->dc", normalized_input, grad_mixed, preferred_element_type=jnp.float32
    )
    grad_normed = unit_sum(
        jnp.einsum("tc,dc->td", grad_mixed, qkv_back[:, 0, :], preferred_element_type=jnp.float32)
    )
    grad_gain_one, grad_input_norm = norm_back(
        inputs_f, inv_first, gain_one_back.astype(jnp.float32), grad_normed
    )
    grad_inputs = grad_middle + grad_input_norm
    grad_qkv_mine, grad_bias_qk_mine, grad_bias_v_mine, grad_gain_one_mine, grad_out_mine = (
        lax.psum_scatter(grad_qkv_w[:, None, :], ("seq", "ctx"), scatter_dimension=0, tiled=True),
        lax.psum_scatter(
            grad_bias[None, :split_at], ("seq", "ctx"), scatter_dimension=1, tiled=True
        ),
        lax.psum_scatter(
            grad_bias[None, split_at:], ("seq", "ctx"), scatter_dimension=1, tiled=True
        ),
        lax.psum_scatter(grad_gain_one, ("seq", "ctx"), scatter_dimension=0, tiled=True),
        lax.psum_scatter(grad_out_w[None], ("seq", "ctx"), scatter_dimension=2, tiled=True),
    )
    grad_gate_mine, grad_up_mine, grad_down_mine, grad_gain_two_mine = (
        lax.psum_scatter(grad_gate_w, ("seq", "ctx"), scatter_dimension=0, tiled=True),
        lax.psum_scatter(grad_up_w, ("seq", "ctx"), scatter_dimension=0, tiled=True),
        lax.psum_scatter(grad_down, ("seq", "ctx"), scatter_dimension=1, tiled=True),
        lax.psum_scatter(grad_gain_two, ("seq", "ctx"), scatter_dimension=0, tiled=True),
    )
    return (
        output.astype(jnp.bfloat16)[None],
        grad_inputs.astype(jnp.bfloat16)[None],
        grad_qkv_mine,
        grad_bias_qk_mine,
        grad_bias_v_mine,
        grad_gain_one_mine,
        grad_out_mine,
        grad_gate_mine,
        grad_up_mine,
        grad_down_mine,
        grad_gain_two_mine,
    )


def solution(mesh):
    return jax.shard_map(
        shards,
        mesh=mesh,
        in_specs=(
            P("seq", "ctx", None),
            P("seq", "ctx"),
            P(("seq", "ctx"), "tp", None),
            P("tp", ("seq", "ctx")),
            P(("seq", "ctx")),
            P("tp", None, ("seq", "ctx")),
            P(("seq", "ctx"), "tp"),
            P(("seq", "ctx"), "tp"),
            P("tp", ("seq", "ctx")),
            P(("seq", "ctx")),
            P("seq", "ctx", None),
        ),
        out_specs=(
            P("seq", "ctx", None),
            P("seq", "ctx", None),
            P(("seq", "ctx"), "tp", None),
            P("tp", ("seq", "ctx")),
            P("tp", ("seq", "ctx")),
            P(("seq", "ctx")),
            P("tp", None, ("seq", "ctx")),
            P(("seq", "ctx"), "tp"),
            P(("seq", "ctx"), "tp"),
            P("tp", ("seq", "ctx")),
            P(("seq", "ctx")),
        ),
        check_vma=False,
    )
```

profile of v0, /device:TPU:8, one launch (start us, length us, event | category | flops | bytes accessed | tf_op | source)
XLA Modules:
  0.0 1781.3 jit_solution(15019593235568705743)
XLA Ops:
  15.1 125.9 %all-reduce.17 = (bf16[896]{0:T(1024)(128)(2,1)S(1)}, bf16[576]{0:T(1024)(128)(2,1)S(1)}, bf16[896]{0:T(1024)(128)(2,1)S(1)}) all-reduce(bf16[896]{0:T(1024)(128)(2,1)S(1)} %dynamic-update-slice, bf16[576]{0:T(1024)(128)(2,1)S(1)} %dynamic-update-slice.1, ...), channel_id=1, replica_groups=mesh['seq'=2,'ctx'=32,'tp'=2] {'seq','ctx'}, use_global_device_ids=true, to_apply=%add | all-reduce | flops 2368 | bytes 9472
  141.8 96.1 %all_gather.36 = bf16[896,1,576]{2,1,0:T(2,128)(2,1)S(1)} all-gather(bf16[14,1,576]{2,1,0:T(2,128)(2,1)S(1)} %copy.52), channel_id=1, replica_groups=mesh['seq'=2,'ctx'=32,'tp'=2] {'seq','ctx'}, dimensions={0}, use_global_device_ids=true | all-gather | bytes 1048320 | tf_op jit(solution)/shard_map/all_gather | solution.py:96
  244.9 83.1 %all_gather.39 = bf16[1,448,896]{1,0,2:T(2,128)(2,1)S(1)} all-gather(bf16[1,448,14]{1,0,2:T(2,128)(2,1)S(1)} %copy.55), channel_id=1, replica_groups=mesh['seq'=2,'ctx'=32,'tp'=2] {'seq','ctx'}, dimensions={2}, use_global_device_ids=true | all-gather | bytes 815360 | tf_op jit(solution)/shard_map/all_gather | solution.py:99
  334.0 70.2 %while.28 = (s32[]{:T(128)}, f32[7,256]{1,0:T(8,128)S(1)}, f32[7,256]{1,0:T(8,128)S(1)}, f32[7,256,64]{1,2,0:T(8,128)S(1)}, s32[16]{0:T(128)S(1)}, /*index=5*/s3...) while((s32[]{:T(128)}, f32[7,256]{1,0:T(8,128)S(1)}, ...), condition=%wide.region_7.8_spmd.clone, body=%wide.region_2.7_spmd.clone.sunk | while | flops 247435520 | bytes 13200715 | solution.py:62
  337.2 3.7 conditional.6
  344.1 3.7 conditional.6
  351.1 3.7 conditional.6
  358.0 3.7 conditional.6
  364.9 3.7 conditional.6
  409.5 76.7 %all-reduce.25.cloned.1.call-done = bf16[256,896]{1,0:T(8,128)(2,1)} async-done(((bf16[256,896]{1,0:T(8,128)(2,1)}), bf16[256,896]{1,0:T(8,128)(2,1)}) %all-reduce.25.cloned.1.call-update) | async-done | bytes 458768 | tf_op jit(solution)/shard_map/psum | solution.py:67
  488.7 75.9 %all-gather.10.cloned.1.call-done = bf16[64,14,2432]{2,1,0:T(8,128)(2,1)} async-done(((bf16[1,14,2432]{2,1,0:T(8,128)(2,1)}), bf16[64,14,2432]{2,1,0:T(8,128)(2,1)}) %all-gather.10.cloned.1.call-update) | async-done | bytes 4358160 | tf_op jit(solution)/shard_map/all_gather | solution.py:102
  564.5 7.2 reshape.291
  571.8 101.3 %all-gather.12.cloned.1.call-done = bf16[64,14,2432]{2,1,0:T(8,128)(2,1)} async-done(((bf16[1,14,2432]{2,1,0:T(8,128)(2,1)}), bf16[64,14,2432]{2,1,0:T(8,128)(2,1)}) %all-gather.12.cloned.1.call-update) | async-done | bytes 4358160 | tf_op jit(solution)/shard_map/all_gather | solution.py:103
  673.1 7.3 reshape.293
  680.3 5.3 fusion.104
  688.7 93.1 %all-gather.14.cloned.1.call-done = bf16[64,14,2432]{2,1,0:T(8,128)(2,1)} async-done(((bf16[1,14,2432]{2,1,0:T(8,128)(2,1)}), bf16[64,14,2432]{2,1,0:T(8,128)(2,1)}) %all-gather.14.cloned.1.call-update) | async-done | bytes 4358160 | tf_op jit(solution)/shard_map/all_gather | solution.py:104
  781.8 7.3 reshape.295
  789.1 6.5 multiply_convert_fusion
  795.6 4.7 fusion.105
  800.3 4.6 fusion.38
  805.2 34.7 %all-reduce.27.cloned.1.call-done = bf16[256,896]{1,0:T(8,128)(2,1)} async-done(((bf16[256,896]{1,0:T(8,128)(2,1)}), bf16[256,896]{1,0:T(8,128)(2,1)}) %all-reduce.27.cloned.1.call-update) | async-done | bytes 458768 | tf_op jit(solution)/shard_map/psum | solution.py:67
  846.5 106.2 %while.29 = (s32[]{:T(128)}, f32[7,256,64]{1,2,0:T(8,128)S(1)}, f32[8192,128]{0,1:T(8,128)}, s32[16]{0:T(128)S(1)}, s32[]{:T(128)}, /*index=5*/s32[]{:T(128)}, s...) while((s32[]{:T(128)}, f32[7,256,64]{1,2,0:T(8,128)S(1)}, ...), condition=%wide.region_17.18_spmd.clone, body=%wide.region_14.17_spmd.clone.sunk | while | flops 598999808 | bytes 20808068 | solution.py:62
  849.7 11.0 conditional.7
  863.9 10.9 conditional.7
  878.0 10.9 conditional.7
  892.1 10.9 conditional.7
  906.2 10.9 conditional.7
  952.7 3.7 convert_element_type.160
  956.5 5.0 convolution_convert_fusion
  961.6 4.9 fusion.77
  966.6 187.4 %reduce-scatter.10.cloned.1.call-done = bf16[256,128]{0,1:T(8,128)(2,1)} async-done(((bf16[8192,128]{0,1:T(8,128)(2,1)}), bf16[256,128]{0,1:T(8,128)(2,1)}) %reduce-scatter.10.cloned.1.call-update) | async-done | bytes 65552 | tf_op jit(solution)/shard_map/reduce_scatter | solution.py:274
  1159.5 6.2 fusion.107
  1165.7 4.8 fusion.106
  1177.4 5.7 copy.58
  1183.2 181.2 %fusion.97 = (f32[16,2432]{1,0:T(8,128)S(1)}, f32[16,2432]{1,0:T(8,128)S(1)}, f32[2432,16]{0,1:T(8,128)}) fusion(f32[896,2432]{1,0:T(8,128)} %fusion.106, f32[896,2432]{1,0:T(8,128)} %fusion.107, f32[2432,896]{0,1:T(8,128)} %fusion.77), kind=kCustom, calls=%all-reduce-scatter.3 | all-reduce-scatter fusion | flops 7471105 | bytes 26616320
  1368.2 4.1 collective-permute-start.23
  1372.3 23.5 %collective-permute-start.15 = (f32[14,2432]{1,0:T(8,128)S(1)}, f32[14,2432]{1,0:T(8,128)S(1)}, u32[]{:S(2)}, u32[]{:S(2)}) collective-permute-start(f32[14,2432]{1,0:T(8,128)S(1)} %slice.107), channel_id=1, source_target_pairs={{0,16},{2,18},{4,20},{6,22},{8,24},{10,26},{12,28},{14,30},{16,32}... | collective-permute-start | bytes 408584
  1395.9 6.2 collective-permute-start.7
  1406.0 4.3 collective-permute-start.3
  1418.0 3.7 collective-permute-start.14
  1421.7 4.4 collective-permute-start.13
  1428.6 5.1 collective-permute-start.11
  1448.4 5.2 collective-permute-start.19
  1457.7 3.7 collective-permute-start.16
  1463.4 9.3 concatenate.41
  1472.7 15.5 concatenate.42
  1488.2 15.4 concatenate.43
  1509.1 256.2 %all-reduce.15 = (f32[1,512]{1,0:T(1,128)S(1)}, f32[1,64]{1,0:T(1,128)S(1)}, f32[896]{0:T(1024)S(1)}, f32[896]{0:T(1024)S(1)}) all-reduce(f32[1,512]{1,0:T(1,128)S(1)} %bitcast.235, f32[1,64]{1,0:T(1,128)S(1)} %slice_bitcast_fusion.9, f32[896]{0:T(1024)S(1)} %get-tuple-element.449, ...), channel_id=4, replica_groups=mesh['seq'=2,'ctx'=32,'tp'=2] {'seq','ctx'}, use_global_device_ids=true, to_apply=%region_23.24.clone | all-reduce | flops 2368 | bytes 18944
  (410 shorter events, 181.4 us)
Async XLA Ops:
  8.0 233.4 %copy-start = (bf16[1,256,896]{2,1,0:T(8,128)(2,1)S(1)}, bf16[1,256,896]{2,1,0:T(8,128)(2,1)}, u32[]{:S(2)}) copy-start(bf16[1,256,896]{2,1,0:T(8,128)(2,1)} %param.19) | copy-start | bytes 1376260
  8.0 324.1 %all-gather.8.cloned.1.call-start = ((), (), s32[]{:S(2)}) async-start(), calls=%async_computation.1 | async-start | bytes 2162688 | tf_op jit(solution)/shard_map/all_gather | solution.py:158
  141.8 101.5 %copy-start.40 = (s32[1,256]{1,0:T(1,128)S(1)}, s32[1,256]{1,0:T(1,128)}, u32[]{:S(2)}) copy-start(s32[1,256]{1,0:T(1,128)} %param.20) | copy-start | bytes 3076
  244.2 242.0 %all-reduce.25.cloned.1.call-start = ((), (), s32[]{:S(2)}) async-start(), calls=%async_computation.2 | async-start | bytes 917504 | tf_op jit(solution)/shard_map/psum | solution.py:67
  404.2 83.2 %copy-start.2 = (bf16[16,512,128]{1,2,0:T(8,128)(2,1)}, bf16[16,512,128]{1,2,0:T(8,128)(2,1)S(1)}, u32[]{:S(2)}) copy-start(bf16[16,512,128]{1,2,0:T(8,128)(2,1)S(1)} %get-tuple-element.821) | copy-start | bytes 6291460
  407.5 157.1 %all-gather.10.cloned.1.call-start = ((), (), s32[]{:S(2)}) async-start(), calls=%async_computation.5 | async-start | bytes 5058560 | tf_op jit(solution)/shard_map/all_gather | solution.py:102
  408.1 265.0 %all-gather.12.cloned.1.call-start = ((), (), s32[]{:S(2)}) async-start(), calls=%async_computation.6 | async-start | bytes 5058560 | tf_op jit(solution)/shard_map/all_gather | solution.py:103
  408.6 373.2 %all-gather.14.cloned.1.call-start = ((), (), s32[]{:S(2)}) async-start(), calls=%async_computation.7 | async-start | bytes 5058560 | tf_op jit(solution)/shard_map/all_gather | solution.py:104
  409.2 430.7 %all-reduce.27.cloned.1.call-start = ((), (), s32[]{:S(2)}) async-start(), calls=%async_computation.3 | async-start | bytes 917504 | tf_op jit(solution)/shard_map/psum | solution.py:67
  688.7 100.4 %copy-start.4 = (bf16[1,256,896]{2,1,0:T(8,128)(2,1)S(1)}, bf16[1,256,896]{2,1,0:T(8,128)(2,1)}, u32[]{:S(2)}) copy-start(bf16[1,256,896]{2,1,0:T(8,128)(2,1)} %param.29) | copy-start | bytes 1376260
  804.9 349.1 %reduce-scatter.10.cloned.1.call-start = ((), (), s32[]{:S(2)}) async-start(), calls=%async_computation.4 | async-start | bytes 2162688 | tf_op jit(solution)/shard_map/reduce_scatter | solution.py:274
  841.4 329.1 %copy-start.39 = (f32[256]{0:T(256)}, f32[256]{0:T(256)S(1)}, u32[]{:S(2)}) copy-start(f32[256]{0:T(256)S(1)} %broadcast_multiply_fusion.2) | copy-start | bytes 3076
  956.5 551.2 %all-reduce.31.cloned.1.call-start = ((), (), s32[]{:S(2)}) async-start(), calls=%async_computation.9 | async-start | bytes 1835008 | tf_op jit(solution)/shard_map/psum | solution.py:67
  966.6 192.8 %copy-start.7 = (bf16[256,7,64]{0,2,1:T(8,128)(2,1)}, bf16[256,7,64]{0,2,1:T(8,128)(2,1)S(1)}, u32[]{:S(2)}) copy-start(bf16[256,7,64]{0,2,1:T(8,128)(2,1)S(1)} %fusion.76) | copy-start | bytes 688132
  1159.1 611.8 %all-reduce.29.cloned.1.call-start = ((), (), s32[]{:S(2)}) async-start(), calls=%async_computation.8 | async-start | bytes 8257536
  1364.4 98.9 %copy-start.13 = (f32[16,2432]{1,0:T(8,128)}, f32[16,2432]{1,0:T(8,128)S(1)}, u32[]{:S(2)}) copy-start(f32[16,2432]{1,0:T(8,128)S(1)} %get-tuple-element.513) | copy-start | bytes 466948
  1364.4 99.0 %copy-start.12 = (f32[16,2432]{1,0:T(8,128)}, f32[16,2432]{1,0:T(8,128)S(1)}, u32[]{:S(2)}) copy-start(f32[16,2432]{1,0:T(8,128)S(1)} %get-tuple-element.514) | copy-start | bytes 466948
  1364.4 47.9 %collective-permute-start.6 = (f32[16,2432]{1,0:T(8,128)S(1)}, f32[16,2432]{1,0:T(8,128)S(1)}, u32[]{:S(2)}, u32[]{:S(2)}) collective-permute-start(f32[16,2432]{1,0:T(8,128)S(1)} %get-tuple-element.513), channel_id=1, source_target_pairs={{0,14},{2,16},{4,18},{6,20},{8,22},{10,24},{12,26},{14,28},{16,30}... | collective-permute-start | bytes 466952
  1368.2 35.8 %collective-permute-start.23 = (f32[2432,14]{0,1:T(8,128)S(1)}, f32[2432,14]{0,1:T(8,128)S(1)}, u32[]{:S(2)}, u32[]{:S(2)}) collective-permute-start(f32[2432,14]{0,1:T(8,128)S(1)} %slice.108), channel_id=1, source_target_pairs={{0,16},{2,18},{4,20},{6,22},{8,24},{10,26},{12,28},{14,30},{16,32}... | collective-permute-start | bytes 408584
  1372.3 33.6 %collective-permute-start.15 = (f32[14,2432]{1,0:T(8,128)S(1)}, f32[14,2432]{1,0:T(8,128)S(1)}, u32[]{:S(2)}, u32[]{:S(2)}) collective-permute-start(f32[14,2432]{1,0:T(8,128)S(1)} %slice.107), channel_id=1, source_target_pairs={{0,16},{2,18},{4,20},{6,22},{8,24},{10,26},{12,28},{14,30},{16,32}... | collective-permute-start | bytes 408584
  1395.9 14.4 collective-permute-start.7
  1402.1 13.6 collective-permute-start.5
  1404.0 59.3 %copy-start.19 = (f32[2432,14]{0,1:T(8,128)}, f32[2432,14]{0,1:T(8,128)S(1)}, u32[]{:S(2)}) copy-start(f32[2432,14]{0,1:T(8,128)S(1)} %collective-permute-done.23) | copy-start | bytes 408580
  1404.0 14.0 collective-permute-start.4
  1406.0 57.4 %copy-start.21 = (f32[14,2432]{1,0:T(8,128)}, f32[14,2432]{1,0:T(8,128)S(1)}, u32[]{:S(2)}) copy-start(f32[14,2432]{1,0:T(8,128)S(1)} %collective-permute-done.15) | copy-start | bytes 408580
  1406.0 15.8 collective-permute-start.3
  1410.3 53.0 %copy-start.22 = (f32[14,2432]{1,0:T(8,128)}, f32[14,2432]{1,0:T(8,128)S(1)}, u32[]{:S(2)}) copy-start(f32[14,2432]{1,0:T(8,128)S(1)} %collective-permute-done.7) | copy-start | bytes 408580
  1410.3 15.9 collective-permute-start.2
  1412.2 51.1 %copy-start.20 = (f32[16,2432]{1,0:T(8,128)}, f32[16,2432]{1,0:T(8,128)S(1)}, u32[]{:S(2)}) copy-start(f32[16,2432]{1,0:T(8,128)S(1)} %collective-permute-done.6) | copy-start | bytes 466948
  1412.3 16.3 collective-permute-start.1
  1415.6 47.7 %copy-start.23 = (f32[16,2432]{1,0:T(8,128)}, f32[16,2432]{1,0:T(8,128)S(1)}, u32[]{:S(2)}) copy-start(f32[16,2432]{1,0:T(8,128)S(1)} %collective-permute-done.5) | copy-start | bytes 466948
  1415.7 18.1 %collective-permute-start = (f32[16,2432]{1,0:T(8,128)S(1)}, f32[16,2432]{1,0:T(8,128)S(1)}, u32[]{:S(2)}, u32[]{:S(2)}) collective-permute-start(f32[16,2432]{1,0:T(8,128)S(1)} %get-tuple-element.513), channel_id=1, source_target_pairs={{0,2},{2,4},{4,6},{6,8},{8,10},{10,12},{12,14},{14,16},{16,18},{18... | collective-permute-start | bytes 466952
  1418.0 45.4 %copy-start.24 = (f32[16,2432]{1,0:T(8,128)}, f32[16,2432]{1,0:T(8,128)S(1)}, u32[]{:S(2)}) copy-start(f32[16,2432]{1,0:T(8,128)S(1)} %collective-permute-done.4) | copy-start | bytes 466948
  1418.0 17.7 collective-permute-start.14
  1421.7 41.6 %copy-start.25 = (f32[16,2432]{1,0:T(8,128)}, f32[16,2432]{1,0:T(8,128)S(1)}, u32[]{:S(2)}) copy-start(f32[16,2432]{1,0:T(8,128)S(1)} %collective-permute-done.3) | copy-start | bytes 466948
  1421.7 15.9 collective-permute-start.13
  1426.2 14.3 collective-permute-start.12
  1428.6 14.9 collective-permute-start.11
  1433.7 12.5 collective-permute-start.10
  1435.7 12.8 collective-permute-start.9
  1437.7 16.0 collective-permute-start.8
  1440.5 15.1 collective-permute-start.22
  1443.5 14.1 collective-permute-start.21
  1446.3 41.9 %collective-permute-start.20 = (f32[2432,16]{0,1:T(8,128)}, f32[2432,16]{0,1:T(8,128)}, u32[]{:S(2)}, u32[]{:S(2)}) collective-permute-start(f32[2432,16]{0,1:T(8,128)} %get-tuple-element.515), channel_id=1, source_target_pairs={{0,10},{2,12},{4,14},{6,16},{8,18},{10,20},{12,22},{14,24},{16,26}... | collective-permute-start | bytes 466952
  1448.4 39.7 %collective-permute-start.19 = (f32[2432,16]{0,1:T(8,128)}, f32[2432,16]{0,1:T(8,128)}, u32[]{:S(2)}, u32[]{:S(2)}) collective-permute-start(f32[2432,16]{0,1:T(8,128)} %get-tuple-element.515), channel_id=1, source_target_pairs={{0,8},{2,10},{4,12},{6,14},{8,16},{10,18},{12,20},{14,22},{16,24},... | collective-permute-start | bytes 466952
  1453.7 34.5 %collective-permute-start.18 = (f32[2432,16]{0,1:T(8,128)}, f32[2432,16]{0,1:T(8,128)}, u32[]{:S(2)}, u32[]{:S(2)}) collective-permute-start(f32[2432,16]{0,1:T(8,128)} %get-tuple-element.515), channel_id=1, source_target_pairs={{0,6},{2,8},{4,10},{6,12},{8,14},{10,16},{12,18},{14,20},{16,22},{... | collective-permute-start | bytes 466952
  1455.7 32.5 %collective-permute-start.17 = (f32[2432,16]{0,1:T(8,128)}, f32[2432,16]{0,1:T(8,128)}, u32[]{:S(2)}, u32[]{:S(2)}) collective-permute-start(f32[2432,16]{0,1:T(8,128)} %get-tuple-element.515), channel_id=1, source_target_pairs={{0,4},{2,6},{4,8},{6,10},{8,12},{10,14},{12,16},{14,18},{16,20},{1... | collective-permute-start | bytes 466952
  1457.7 30.5 %collective-permute-start.16 = (f32[2432,16]{0,1:T(8,128)}, f32[2432,16]{0,1:T(8,128)}, u32[]{:S(2)}, u32[]{:S(2)}) collective-permute-start(f32[2432,16]{0,1:T(8,128)} %get-tuple-element.515), channel_id=1, source_target_pairs={{0,2},{2,4},{4,6},{6,8},{8,10},{10,12},{12,14},{14,16},{16,18},{18... | collective-permute-start | bytes 466952
  (26 other events, 330.7 us)
Sparse Core Ops, SparseCore 0:
  244.3 50.0 all-gather.7
  407.6 78.5 all-reduce.24
  805.1 34.8 all-reduce.26
  956.6 197.3 reduce-scatter.9
  1159.3 44.9 all-reduce.30
  1206.8 551.4 all-reduce.28
Sparse Core Ops, SparseCore 1:
  409.8 154.7 all-gather.9
  566.2 106.8 all-gather.11
  674.8 107.0 all-gather.13
where the time goes:
time: 1810 us; the launch traced here: 1780 us
  blocking collectives  743 us (41%)
  waiting for transfers between devices  571 us (32%)
  local copies, waits for them, and re-layouts  133 us (7%)
  starting transfers between devices  96.3 us (5%)
  loops' own time  94.9 us (5%)
  matrix products  87.7 us (5%)
  other arithmetic  35.6 us (2%)
  between operations  20 us (1%)
    unnamed x3, blocking collectives  563 us
    reduce_scatter x1, waiting for transfers between devices, shards(): lax.psum_scatter(grad_kv.astype(jnp.bfloat16), 'ctx', scatter_dimension=0...  187 us
    psum x3, waiting for transfers between devices, unit_sum(): return lax.psum(partial_sum.astype(jnp.bfloat16), 'tp').astype(jnp.float32)  111 us
    all_gather x1, waiting for transfers between devices, shards(): lax.all_gather(up_weight, ('seq', 'ctx'), axis=0, tiled=True)  101 us
    all_gather x1, blocking collectives, shards(): lax.all_gather(query_key_value_weight, ('seq', 'ctx'), axis=0, tiled=True)  96.1 us
    unnamed x25, starting transfers between devices  95.5 us
    all_gather x1, waiting for transfers between devices, shards(): lax.all_gather(down_weight, ('seq', 'ctx'), axis=1, tiled=True)  93.1 us
    another operation x2, loops' own time, key_blocks(): running, unused = lax.scan(scan_body, running, (pieces, offsets))  84 us
  transfers between devices with their start and end apart: 33, of which 7 were waited for; matrix products, arithmetic and copies ran while one was open for 17% of the time, Pallas kernels for 0%

commit v1 on v0

v1 whole, which is shorter than its diff:
```python
import jax
import jax.numpy as jnp
import numpy as np
from jax import lax
from jax.experimental import pallas as pl
from jax.experimental.pallas import tpu as pltpu
from jax.sharding import PartitionSpec as P

MESH_ID = pl.DeviceIdType.MESH
ANY = pl.ANY
VMEM = pltpu.VMEM


class Place:
    def __init__(self):
        self.seq = lax.axis_index("seq")
        ctx = lax.axis_index("ctx")
        self.ctx = ctx
        self.tp = lax.axis_index("tp")
        self.core = ctx % 2
        core = self.core
        y, z = ctx // 8, (ctx // 2) % 4
        self.a = y * (1 - core) + z * core
        self.b = z * (1 - core) + y * core
        self.stride_a = 8 - 6 * core
        self.stride_b = 2 + 6 * core
        self.a_next = self.peer(1, 0)
        self.a_prev = self.peer(3, 0)
        self.b_next = self.peer(0, 1)
        self.b_prev = self.peer(0, 3)
        self.other_core = {"ctx": ctx + 1 - 2 * core}
        self.other_seq = {"seq": 1 - self.seq}
        self.mirror = {"ctx": 31 - ctx}
        self.other_tp = {"tp": 1 - self.tp}

    def peer(self, da, db):
        a, b = (self.a + da) % 4, (self.b + db) % 4
        return {"ctx": a * self.stride_a + b * self.stride_b + self.core}


def greet(peers):
    barrier = pltpu.get_barrier_semaphore()
    for peer in peers:
        pl.semaphore_signal(barrier, inc=1, device_id=peer, device_id_type=MESH_ID)
    pl.semaphore_wait(barrier, len(peers))


def remote(src, dst, send, recv, index, peer):
    return pltpu.make_async_remote_copy(
        src_ref=src,
        dst_ref=dst,
        send_sem=send.at[index],
        recv_sem=recv.at[index],
        device_id=peer,
        device_id_type=MESH_ID,
    )


GATHER_SEMS = 13


class Gather:
    def __init__(self, place, own, full, send, recv, local):
        self.p, self.own, self.full = place, own, full
        self.send, self.recv, self.local = send, recv, local
        self.pair = full.shape[3] == 2
        self.started = []

    def go(self, src, dst, index, peer):
        copy = remote(src, dst, self.send, self.recv, index, peer)
        copy.start()
        self.started.append(copy)

    def got(self, ref, index):
        remote(ref, ref, self.send, self.recv, index, self.p.a_next).wait_recv()

    def half(self, b, a, which):
        ref = self.full.at[self.p.core, b, a]
        if self.pair:
            return ref.at[which]
        rows = self.full.shape[4] // 2
        return ref.at[0, pl.ds(which * rows, rows)]

    def begin(self):
        p = self.p
        slot = self.full.at[p.core, p.b, p.a, p.seq if self.pair else 0]
        self.mine = pltpu.make_async_copy(self.own, slot, self.local)
        self.mine.start()
        if self.pair:
            self.go(self.own, slot, 0, p.other_seq)

    def first(self):
        p = self.p
        self.mine.wait()
        if self.pair:
            self.got(self.full.at[p.core, p.b, p.a, 1 - p.seq], 0)
        block = self.full.at[p.core, p.b, p.a]
        self.go(block, block, 1, p.a_next)
        self.go(block, block, 2, p.a_prev)

    def second(self):
        p = self.p
        down, up = (p.a + 3) % 4, (p.a + 1) % 4
        self.got(self.full.at[p.core, p.b, down], 1)
        half = self.half(p.b, down, 0)
        self.go(half, half, 3, p.a_next)
        self.got(self.full.at[p.core, p.b, up], 2)
        half = self.half(p.b, up, 1)
        self.go(half, half, 4, p.a_prev)

    def third(self):
        p = self.p
        far = (p.a + 2) % 4
        self.got(self.half(p.b, far, 0), 3)
        self.got(self.half(p.b, far, 1), 4)
        block = self.full.at[p.core, p.b]
        self.go(block, block, 5, p.b_next)
        self.go(block, block, 6, p.b_prev)
        self.go(block, block, 9, p.other_core)

    def fourth(self):
        p = self.p
        down, up = (p.b + 3) % 4, (p.b + 1) % 4
        block = self.full.at[p.core, down]
        self.got(block, 5)
        half = self.full.at[p.core, down, pl.ds(0, 2)]
        self.go(half, half, 7, p.b_next)
        self.go(block, block, 10, p.other_core)
        block = self.full.at[p.core, up]
        self.got(block, 6)
        half = self.full.at[p.core, up, pl.ds(2, 2)]
        self.go(half, half, 8, p.b_prev)
        self.go(block, block, 11, p.other_core)

    def fifth(self):
        p = self.p
        far = (p.b + 2) % 4
        self.got(self.full.at[p.core, far, pl.ds(0, 2)], 7)
        self.got(self.full.at[p.core, far, pl.ds(2, 2)], 8)
        block = self.full.at[p.core, far]
        self.go(block, block, 12, p.other_core)

    def finish(self):
        p = self.p
        for index, step in ((9, 0), (10, 3), (11, 1), (12, 2)):
            self.got(self.full.at[1 - p.core, (p.a + step) % 4], index)
        for copy in self.started:
            copy.wait_send()

    def peers(self):
        p = self.p
        found = [p.a_next, p.a_prev, p.b_next, p.b_prev, p.other_core]
        return found + ([p.other_seq] if self.pair else [])


def add_into(target, extra, count):
    def body(k, carry):
        total = target[k].astype(jnp.float32) + extra[k].astype(jnp.float32)
        target[k] = total.astype(target.dtype)
        return carry

    lax.fori_loop(0, count, body, 0)


SCATTER_SEMS = 13


class Scatter:
    @staticmethod
    def scratch(seqs, rows, width):
        bf16 = jnp.bfloat16
        half = (1, rows, width) if seqs == 2 else (1, rows // 2, width)
        return [
            VMEM((4, 4, seqs, rows, width), bf16),
            VMEM((2, 2, seqs, rows, width), bf16),
            VMEM((2, 4, seqs, rows, width), bf16),
            VMEM((2,) + half, bf16),
            VMEM((2, seqs, rows, width), bf16),
            VMEM((1, rows, width), bf16),
            pltpu.SemaphoreType.DMA((SCATTER_SEMS,)),
            pltpu.SemaphoreType.DMA((SCATTER_SEMS,)),
        ]

    def __init__(self, place, part, scratch):
        self.p, self.part = place, part
        self.sums, self.far_b, self.near_b, self.far_a, self.near_a, self.across, self.send, self.recv = scratch
        self.seqs, self.rows = part.shape[3], part.shape[4]
        self.started = []

    go = Gather.go
    got = Gather.got

    def half(self, b, a, which):
        ref = self.sums.at[b, a]
        if self.seqs == 2:
            return ref.at[pl.ds(which, 1)]
        rows = self.rows // 2
        return ref.at[:, pl.ds(which * rows, rows)]

    def begin(self):
        p = self.p
        for step in (2, 1, 3, 0):
            slot = (p.a + step) % 4
            self.go(self.part.at[1 - p.core, slot], self.sums.at[slot], step, p.other_core)

    def add_core(self, step):
        p = self.p
        slot = (p.b + step) % 4
        self.got(self.sums.at[slot], step)
        for a in range(4):
            add_into(self.sums.at[slot, a], self.part.at[p.core, slot, a], self.seqs)

    def first(self):
        p = self.p
        self.add_core(2)
        far = (p.b + 2) % 4
        self.go(self.sums.at[far, pl.ds(0, 2)], self.far_b.at[0], 4, p.b_next)
        self.go(self.sums.at[far, pl.ds(2, 2)], self.far_b.at[1], 5, p.b_prev)

    def second(self):
        p = self.p
        up, down = (p.b + 1) % 4, (p.b + 3) % 4
        self.add_core(1)
        self.add_core(3)
        self.got(self.far_b.at[0], 4)
        for a in range(2):
            add_into(self.sums.at[up, a], self.far_b.at[0, a], self.seqs)
        self.go(self.sums.at[up], self.near_b.at[0], 6, p.b_next)
        self.got(self.far_b.at[1], 5)
        for a in range(2):
            add_into(self.sums.at[down, a + 2], self.far_b.at[1, a], self.seqs)
        self.go(self.sums.at[down], self.near_b.at[1], 7, p.b_prev)
        self.add_core(0)

    def third(self):
        p = self.p
        for side in range(2):
            self.got(self.near_b.at[side], 6 + side)
            for a in range(4):
                add_into(self.sums.at[p.b, a], self.near_b.at[side, a], self.seqs)
        far = (p.a + 2) % 4
        self.go(self.half(p.b, far, 0), self.far_a.at[0], 8, p.a_next)
        self.go(self.half(p.b, far, 1), self.far_a.at[1], 9, p.a_prev)

    def fourth(self):
        p = self.p
        up, down = (p.a + 1) % 4, (p.a + 3) % 4
        self.got(self.far_a.at[0], 8)
        add_into(self.half(p.b, up, 0), self.far_a.at[0], 1)
        self.go(self.sums.at[p.b, up], self.near_a.at[0], 10, p.a_next)
        self.got(self.far_a.at[1], 9)
        add_into(self.half(p.b, down, 1), self.far_a.at[1], 1)
        self.go(self.sums.at[p.b, down], self.near_a.at[1], 11, p.a_prev)

    def fifth(self):
        p = self.p
        for side in range(2):
            self.got(self.near_a.at[side], 10 + side)
            add_into(self.sums.at[p.b, p.a], self.near_a.at[side], self.seqs)
        if self.seqs == 2:
            self.go(self.sums.at[p.b, p.a, pl.ds(1 - p.seq, 1)], self.across, 12, p.other_seq)

    def finish(self, out):
        p = self.p
        if self.seqs == 2:
            self.got(self.across, 12)
            out[...] = self.sums[p.b, p.a, p.seq].astype(jnp.float32) + self.across[0].astype(jnp.float32)
        else:
            out[...] = self.sums[p.b, p.a, 0].astype(jnp.float32)
        for copy in self.started:
            copy.wait_send()

    def peers(self):
        p = self.p
        found = [p.a_next, p.a_prev, p.b_next, p.b_prev, p.other_core]
        return found + ([p.other_seq] if self.seqs == 2 else [])


def gather_blocks(blocks, seqs, collective_id):
    def kernel(*refs):
        n = len(blocks)
        place = Place()
        gathers = [
            Gather(place, refs[k], refs[n + k], refs[2 * n + 3 * k], refs[2 * n + 3 * k + 1], refs[2 * n + 3 * k + 2])
            for k in range(n)
        ]
        greet(gathers[0].peers())
        for stage in ("begin", "first", "second", "third", "fourth", "fifth", "finish"):
            for gather in gathers:
                getattr(gather, stage)()

    scratch = []
    for block in blocks:
        scratch += [pltpu.SemaphoreType.DMA((GATHER_SEMS,))] * 2 + [pltpu.SemaphoreType.DMA]
    return pl.pallas_call(
        kernel,
        out_shape=[jax.ShapeDtypeStruct((2, 4, 4, seqs) + block.shape, block.dtype) for block in blocks],
        in_specs=[pl.BlockSpec(memory_space=ANY)] * len(blocks),
        out_specs=[pl.BlockSpec(memory_space=ANY)] * len(blocks),
        scratch_shapes=scratch,
        compiler_params=pltpu.CompilerParams(
            collective_id=collective_id, has_side_effects=True, vmem_limit_bytes=60 << 20
        ),
    )(*blocks)


def scatter_sum(part, collective_id):
    seqs, rows, width = part.shape[3:]

    def kernel(part_ref, out_ref, *scratch):
        scatter = Scatter(Place(), part_ref, scratch)
        greet(scatter.peers())
        for stage in ("begin", "first", "second", "third", "fourth", "fifth"):
            getattr(scatter, stage)()
        scatter.finish(out_ref)

    return pl.pallas_call(
        kernel,
        out_shape=jax.ShapeDtypeStruct((rows, width), jnp.float32),
        in_specs=[pl.BlockSpec(memory_space=VMEM)],
        out_specs=pl.BlockSpec(memory_space=VMEM),
        scratch_shapes=Scatter.scratch(seqs, rows, width),
        compiler_params=pltpu.CompilerParams(
            collective_id=collective_id, has_side_effects=True, vmem_limit_bytes=60 << 20
        ),
    )(part)


def swap(arrays, which, collective_id):
    n = len(arrays)

    def kernel(*refs):
        place = Place()
        peer = getattr(place, which)
        greet([peer])
        copies = [remote(refs[k], refs[n + k], refs[2 * n], refs[2 * n + 1], k, peer) for k in range(n)]
        for copy in copies:
            copy.start()
        for copy in copies:
            copy.wait()

    return pl.pallas_call(
        kernel,
        out_shape=[jax.ShapeDtypeStruct(array.shape, array.dtype) for array in arrays],
        in_specs=[pl.BlockSpec(memory_space=ANY)] * n,
        out_specs=[pl.BlockSpec(memory_space=ANY)] * n,
        scratch_shapes=[pltpu.SemaphoreType.DMA((n,))] * 2,
        compiler_params=pltpu.CompilerParams(
            collective_id=collective_id, has_side_effects=True, vmem_limit_bytes=60 << 20
        ),
    )(*arrays)


NEGATIVE = -1e30
HD = 64
ROWS = 896
F32, BF16 = jnp.float32, jnp.bfloat16


def mm(left, right):
    return jnp.dot(left, right, preferred_element_type=F32)


def mm_nt(left, right):
    return lax.dot_general(left, right, (((1,), (1,)), ((), ())), preferred_element_type=F32)


def slot_of(block):
    core, y, z = block % 2, block // 8, (block // 2) % 4
    a = y * (1 - core) + z * core
    b = z * (1 - core) + y * core
    return core, b, a


def for_blocks(count, step):
    step(0, True)

    def body(block, carry):
        step(block, False)
        return carry

    lax.fori_loop(1, count - 1, body, 0)

    @pl.when(count > 1)
    def _():
        step(count - 1, True)


def segment(ctx, index):
    if index == 0:
        return ctx + 1, ctx * 256
    return 32 - ctx, (31 - ctx) * 256 + 128


def visible_of(block, first_row, doc_start, lanes):
    key = lax.broadcasted_iota(jnp.int32, (256, lanes.size), 0) + block * 256
    row = (lax.broadcasted_iota(jnp.int32, (256, lanes.size), 1) + lanes.start) % 128 + first_row
    return (key <= row) & (key >= doc_start)


def attend(ctx, kv_ref, q_ref, doc_ref, out_ref, lse_ref, m_ref, l_ref, acc_ref, chunk):
    for index in range(2):
        count, first_row = segment(ctx, index)
        m_ref[...] = jnp.full(m_ref.shape, NEGATIVE, F32)
        l_ref[...] = jnp.zeros(l_ref.shape, F32)
        acc_ref[...] = jnp.zeros(acc_ref.shape, F32)

        def step(block, masked):
            core, b, a = slot_of(block)
            kv = kv_ref[core, b, a, 0]
            keys, values_t = kv[:, :HD], kv[:, HD:].T
            for start in range(0, ROWS, chunk):
                lanes = pl.ds(start, min(chunk, ROWS - start))
                scores = mm(keys, q_ref[index, :, lanes])
                if masked:
                    doc = doc_ref[:, lanes] if index == 0 else 128
                    scores = jnp.where(visible_of(block, first_row, doc, lanes), scores, NEGATIVE)
                old = m_ref[:, lanes]
                new = jnp.maximum(old, jnp.max(scores, 0, keepdims=True))
                probs = jnp.exp(scores - new)
                keep = jnp.exp(old - new)
                m_ref[:, lanes] = new
                l_ref[:, lanes] = l_ref[:, lanes] * keep + jnp.sum(probs, 0, keepdims=True)
                acc_ref[:, lanes] = acc_ref[:, lanes] * keep + mm(values_t, probs.astype(BF16))

        for_blocks(count, step)
        out_ref[index] = acc_ref[...] / l_ref[...]
        lse_ref[index] = m_ref[...] + jnp.log(l_ref[...])


def attend_back(ctx, kv_ref, q_ref, doc_ref, do_ref, lse_ref, delta_ref, dq_ref, dkv_ref, chunk):
    dq_ref[...] = jnp.zeros(dq_ref.shape, F32)

    def clear(block, carry):
        core, b, a = slot_of(block)
        dkv_ref[core, b, a, 0] = jnp.zeros((256, 128), F32)
        return carry

    lax.fori_loop(0, 32, clear, 0)
    for index in range(2):
        count, first_row = segment(ctx, index)

        def step(block, masked):
            core, b, a = slot_of(block)
            kv = kv_ref[core, b, a, 0]
            keys, values = kv[:, :HD], kv[:, HD:]
            keys_t = keys.T
            dk = dv = jnp.zeros((256, HD), F32)
            for start in range(0, ROWS, chunk):
                lanes = pl.ds(start, min(chunk, ROWS - start))
                q, do = q_ref[index, :, lanes], do_ref[index, :, lanes]
                scores = mm(keys, q)
                if masked:
                    doc = doc_ref[:, lanes] if index == 0 else 128
                    scores = jnp.where(visible_of(block, first_row, doc, lanes), scores, NEGATIVE)
                probs = jnp.exp(scores - lse_ref[index, :, lanes])
                dscores = (probs * (mm(values, do) - delta_ref[index, :, lanes])).astype(BF16)
                dq_ref[index, :, lanes] += mm(keys_t, dscores)
                dk += mm_nt(dscores, q)
                dv += mm_nt(probs.astype(BF16), do)
            dkv_ref[core, b, a, 0] += jnp.concatenate([dk, dv], 1)

        for_blocks(count, step)


D, DPAD, FF_HERE, GROUP, GROUP_Q = 896, 1024, 2432, 576, 448
ATTN_W = GROUP + GROUP_Q + 128
EPS_VALUE = 1e-06
THETA = 1000000.0


def slot_columns():
    index = np.arange(64)
    seq, y, z, core = index // 32, (index // 8) % 4, (index // 2) % 4, index % 2
    a, b = np.where(core == 0, y, z), np.where(core == 0, z, y)
    slot = ((core * 4 + b) * 4 + a) * 2 + seq
    columns = np.full((64, 16), -1)
    columns[slot, :14] = index[:, None] * 14 + np.arange(14)
    return columns.reshape(-1)


def mm_tn(left, right):
    return lax.dot_general(left, right, (((0,), (0,)), ((), ())), preferred_element_type=F32)


def rope_tables(positions):
    exponents = jnp.arange(HD // 2, dtype=F32) * (2.0 / HD)
    freqs = THETA ** (-exponents)
    angles = freqs[:, None] * positions.astype(F32)[None, :]
    angles = jnp.concatenate([angles, angles], 0)
    return jnp.cos(angles), jnp.sin(angles)


def rotate(values, cosine, sine):
    turned = jnp.concatenate([-values[..., 32:, :], values[..., :32, :]], -2)
    return values * cosine + turned * sine


def rotate_back(grads, cosine, sine):
    sined = grads * sine
    return grads * cosine + jnp.concatenate([sined[..., 32:, :], -sined[..., :32, :]], -2)


def norm_back(values, inv_rms, gain, grad_normed):
    scaled = grad_normed * gain
    grad_gain = jnp.sum(grad_normed * values * inv_rms, 1, keepdims=True)
    mean = jnp.sum(scaled * values, 0, keepdims=True) * (1.0 / D)
    return grad_gain, inv_rms * scaled - values * inv_rms**3 * mean


def inv_rms(values):
    return lax.rsqrt(jnp.sum(values * values, 0, keepdims=True) * (1.0 / D) + EPS_VALUE)


def heads_to_lanes(values):
    return values.reshape(7, HD, 128).transpose(1, 0, 2).reshape(HD, ROWS)


def lanes_to_heads(values):
    return values.reshape(HD, 7, 128).transpose(1, 0, 2).reshape(GROUP_Q, 128)


def local_call(kernel, out_shape, inputs, scratch=()):
    return pl.pallas_call(
        kernel,
        out_shape=out_shape,
        in_specs=[pl.BlockSpec(memory_space=VMEM)] * len(inputs),
        out_specs=[pl.BlockSpec(memory_space=VMEM)] * len(out_shape),
        scratch_shapes=list(scratch),
        compiler_params=pltpu.CompilerParams(vmem_limit_bytes=60 << 20),
    )(*inputs)


def shards(
    inputs,
    positions,
    query_key_value_weight,
    query_key_value_bias,
    gain_attn,
    output_weight,
    gate_weight,
    up_weight,
    down_weight,
    gain_ffn,
    cotangent,
):
    me = lax.axis_index("seq") * 32 + lax.axis_index("ctx")
    columns = slot_columns()
    select = jnp.asarray(columns[:, None] == np.arange(D)[None, :], BF16)
    is_bias_row = jnp.asarray((np.arange(DPAD) % 16 == 14)[:, None])

    bias_row = lax.dynamic_update_slice(jnp.zeros((1, GROUP), BF16), query_key_value_bias, (0, 9 * me))
    gains = jnp.stack([gain_attn, gain_ffn], 1)
    attn_row = jnp.concatenate(
        [
            jnp.concatenate([query_key_value_weight[:, 0], bias_row, jnp.zeros((1, GROUP), BF16)], 0),
            jnp.pad(output_weight[0].T, ((0, 2), (0, 0))),
            jnp.pad(gains, ((0, 2), (0, 126))),
        ],
        1,
    )
    ffn_row = jnp.pad(jnp.concatenate([gate_weight, up_weight, down_weight.T], 1), ((0, 2), (0, 0)))
    attn_full, ffn_full = gather_blocks([attn_row, ffn_row], 2, 0)
    attn_full, ffn_full = attn_full.reshape(DPAD, ATTN_W), ffn_full.reshape(DPAD, 3 * FF_HERE)
    w_qkv, w_out = attn_full[:, :GROUP], attn_full[:, GROUP : GROUP + GROUP_Q]
    gain_one = attn_full[:, GROUP + GROUP_Q : GROUP + GROUP_Q + 1].astype(F32)
    gain_two = attn_full[:, GROUP + GROUP_Q + 1 : GROUP + GROUP_Q + 2].astype(F32)
    w_gate, w_up, w_down = (ffn_full[:, k * FF_HERE : (k + 1) * FF_HERE] for k in range(3))

    cosine, sine = rope_tables(positions[0])
    x = mm_nt(select, inputs[0])
    ct_low = mm_nt(select, cotangent[0]).astype(BF16)
    inv_one = inv_rms(x)
    normed = jnp.where(is_bias_row, 1.0, x * inv_one * gain_one).astype(BF16)
    mixed = mm_tn(w_qkv, normed)
    queries = rotate(mixed[:GROUP_Q].reshape(7, HD, 256), cosine, sine).astype(BF16) * BF16(0.125)
    queries = queries.reshape(GROUP_Q, 256)
    keys = rotate(mixed[GROUP_Q : GROUP_Q + HD], cosine, sine).astype(BF16)
    kv = jnp.concatenate([keys, mixed[GROUP_Q + HD :].astype(BF16)], 0).T
    (kv_full,) = gather_blocks([kv], 1, 1)
    (q_far,) = swap([heads_to_lanes(queries[:, 128:])], "mirror", 2)
    q_both = jnp.stack([heads_to_lanes(queries[:, :128]), q_far])
    row = lax.axis_index("ctx") * 256 + jnp.arange(128, dtype=jnp.int32)
    doc_start = jnp.tile((row - positions[0, :128])[None], (1, 7))

    def attend_kernel(*refs):
        attend(lax.axis_index("ctx"), *refs, ROWS)

    attended, lse = local_call(
        attend_kernel,
        [jax.ShapeDtypeStruct((2, HD, ROWS), F32), jax.ShapeDtypeStruct((2, 1, ROWS), F32)],
        [kv_full, q_both, doc_start],
        [VMEM((1, ROWS), F32), VMEM((1, ROWS), F32), VMEM((HD, ROWS), F32)],
    )
    attended_low = attended.astype(BF16)
    (att_far,) = swap([attended_low[1]], "mirror", 3)
    att = jnp.concatenate([lanes_to_heads(attended_low[0]), lanes_to_heads(att_far)], 1)
    branch = mm(w_out, att).astype(BF16)
    (branch_other,) = swap([branch], "other_tp", 4)
    middle = x + (branch.astype(F32) + branch_other.astype(F32))
    inv_two = inv_rms(middle)
    normed_ffn = (middle * inv_two * gain_two).astype(BF16)
    gate, up = mm_tn(normed_ffn, w_gate), mm_tn(normed_ffn, w_up)
    sigmoid = jax.nn.sigmoid(gate)
    hidden = (gate * sigmoid * up).astype(BF16)
    out_part = mm_nt(w_down, hidden).astype(BF16)
    grad_hidden = mm_tn(ct_low, w_down)
    grad_down = mm(ct_low, hidden)
    grad_up_act = (grad_hidden * (gate * sigmoid)).astype(BF16)
    grad_gate_act = (grad_hidden * up * sigmoid * (1.0 + gate * (1.0 - sigmoid))).astype(BF16)
    grad_gate, grad_up = mm(normed_ffn, grad_gate_act), mm(normed_ffn, grad_up_act)
    grad_n = (mm_nt(w_gate, grad_gate_act) + mm_nt(w_up, grad_up_act)).astype(BF16)
    grad_n_other, out_other = swap([grad_n, out_part], "other_tp", 5)
    output = middle + (out_part.astype(F32) + out_other.astype(F32))
    grad_gain_two, grad_norm = norm_back(middle, inv_two, gain_two, grad_n.astype(F32) + grad_n_other.astype(F32))
    grad_middle = ct_low.astype(F32) + grad_norm
    grad_branch = grad_middle.astype(BF16)
    grad_out_w = mm_nt(grad_branch, att)
    grad_att = mm_tn(w_out, grad_branch).astype(BF16)
    (do_far,) = swap([heads_to_lanes(grad_att[:, 128:])], "mirror", 6)
    do_both = jnp.stack([heads_to_lanes(grad_att[:, :128]), do_far])
    delta = jnp.sum(do_both.astype(F32) * attended, 1, keepdims=True)

    def back_kernel(*refs):
        attend_back(lax.axis_index("ctx"), *refs, ROWS)

    grad_q, grad_kv = local_call(
        back_kernel,
        [jax.ShapeDtypeStruct((2, HD, ROWS), F32), jax.ShapeDtypeStruct((2, 4, 4, 1, 256, 128), F32)],
        [kv_full, q_both, doc_start, do_both, lse, delta],
    )
    (dq_far,) = swap([grad_q[1].astype(BF16)], "mirror", 7)
    grad_kv = scatter_sum(grad_kv.astype(BF16), 8).T
    grad_q = jnp.concatenate([lanes_to_heads(grad_q[0]), lanes_to_heads(dq_far).astype(F32)], 1) * 0.125
    grad_q = rotate_back(grad_q.reshape(7, HD, 256), cosine, sine).reshape(GROUP_Q, 256)
    grad_k = rotate_back(grad_kv[:HD], cosine, sine)
    grad_mixed = jnp.concatenate([grad_q, grad_k, grad_kv[HD:]], 0).astype(BF16)
    grad_qkv = mm_nt(normed, grad_mixed)
    grad_normed = mm(w_qkv, grad_mixed).astype(BF16)
    (grad_normed_other,) = swap([grad_normed], "other_tp", 9)
    grad_gain_one, grad_norm = norm_back(
        x, inv_one, gain_one, grad_normed.astype(F32) + grad_normed_other.astype(F32)
    )
    grad_inputs = grad_middle + grad_norm

    part = jnp.concatenate(
        [
            grad_qkv.astype(BF16),
            grad_out_w.astype(BF16),
            jnp.pad(jnp.concatenate([grad_gain_one, grad_gain_two], 1), ((0, 0), (0, 126))).astype(BF16),
            grad_gate.astype(BF16),
            grad_up.astype(BF16),
            grad_down.astype(BF16),
        ],
        1,
    )
    mine = scatter_sum(part.reshape(2, 4, 4, 2, 16, ATTN_W + 3 * FF_HERE), 10)
    ffn = ATTN_W
    return (
        mm_tn(output.astype(BF16), select).astype(BF16)[None],
        mm_tn(grad_inputs.astype(BF16), select).astype(BF16)[None],
        mine[:14, None, :GROUP],
        lax.dynamic_slice(mine, (14, 8 * me), (1, 8)),
        lax.dynamic_slice(mine, (14, 512 + me), (1, 1)),
        mine[:14, GROUP + GROUP_Q],
        mine[:14, GROUP : GROUP + GROUP_Q].T[None],
        mine[:14, ffn : ffn + FF_HERE],
        mine[:14, ffn + FF_HERE : ffn + 2 * FF_HERE],
        mine[:14, ffn + 2 * FF_HERE :].T,
        mine[:14, GROUP + GROUP_Q + 1],
    )


def solution(mesh):
    both = ("seq", "ctx")
    return jax.shard_map(
        shards,
        mesh=mesh,
        in_specs=(
            P("seq", "ctx", None),
            P("seq", "ctx"),
            P(both, "tp", None),
            P("tp", both),
            P(both),
            P("tp", None, both),
            P(both, "tp"),
            P(both, "tp"),
            P("tp", both),
            P(both),
            P("seq", "ctx", None),
        ),
        out_specs=(
            P("seq", "ctx", None),
            P("seq", "ctx", None),
            P(both, "tp", None),
            P("tp", both),
            P("tp", both),
            P(both),
            P("tp", None, both),
            P(both, "tp"),
            P(both, "tp"),
            P("tp", both),
            P(both),
        ),
        check_vma=False,
    )
```

time: 1810 us -> 479 us (0.26); the launches traced: 1780 us -> 471 us
  blocking collectives: 743 us -> 0 us
  waiting for transfers between devices: 571 us -> 0 us
  Pallas kernels: 0 us -> 339 us
  starting transfers between devices: 96.3 us -> 0 us
  loops' own time: 94.9 us -> 0 us
  local copies, waits for them, and re-layouts: 133 us -> 56 us
  matrix products: 87.7 us -> 52.9 us
    unnamed x3 -> x0, blocking collectives: 563 us -> none
    pallas_call x0 -> x13, Pallas kernels: none -> 339 us  [the longest x2 101 us: scatter_sum(): pl.pallas_call(kernel, out_shape=jax.ShapeDtypeStruct((rows, width), jnp....]
    all_gather x4 -> x0, waiting for transfers between devices: 270 us -> none  [the longest x1 101 us: shards(): lax.all_gather(up_weight, ('seq', 'ctx'), axis=0, tiled=True)]
    reduce_scatter x1 -> x0, waiting for transfers between devices: 187 us -> none  [shards(): lax.psum_scatter(grad_kv.astype(jnp.bfloat16), 'ctx', scatter_dimension=0...]
    all_gather x2 -> x0, blocking collectives: 179 us -> none  [the longest x1 96.1 us: shards(): lax.all_gather(query_key_value_weight, ('seq', 'ctx'), axis=0, tiled=True)]
    psum x3 -> x0, waiting for transfers between devices: 111 us -> none  [unit_sum(): return lax.psum(partial_sum.astype(jnp.bfloat16), 'tp').astype(jnp.float32)]
    unnamed x25 -> x0, starting transfers between devices: 95.5 us -> none
    another operation x34 -> x0, loops' own time: 94.9 us -> none  [the longest x2 84 us: key_blocks(): running, unused = lax.scan(scan_body, running, (pieces, offsets))]
  transfers between devices with their start and end apart: 33 -> 0, of which waited for: 7 -> 0; matrix products, arithmetic and copies ran while one was open for 17% -> 0% of each run, Pallas kernels for 0% -> 0%
where the time goes in v1:
time: 479 us; the launch traced here: 471 us
  Pallas kernels  339 us (71%)
  local copies, waits for them, and re-layouts  56 us (12%)
  matrix products  52.9 us (11%)
  other arithmetic  21 us (4%)
    pallas_call x2, Pallas kernels, scatter_sum(): pl.pallas_call(kernel, out_shape=jax.ShapeDtypeStruct((rows, width), jnp....  101 us
    pallas_call x2, Pallas kernels, gather_blocks(): pl.pallas_call(kernel, out_shape=[jax.ShapeDtypeStruct((2, 4, 4, seqs) +...  95.3 us
    pallas_call x7, Pallas kernels, swap(): pl.pallas_call(kernel, out_shape=[jax.ShapeDtypeStruct(array.shape, array...  86.9 us
    pallas_call x2, Pallas kernels, local_call(): pl.pallas_call(kernel, out_shape=out_shape, in_specs=[pl.BlockSpec(memory...  56.3 us
    concatenate x1, local copies, waits for them, and re-layouts, shards(): jnp.concatenate([grad_qkv.astype(BF16), grad_out_w.astype(BF16), jnp.pad(...  28.9 us
    dot_general x7, matrix products, mm_tn(): lax.dot_general(left, right, (((0,), (0,)), ((), ())), preferred_element_...  23.6 us
    dot_general x5, matrix products, mm(): return jnp.dot(left, right, preferred_element_type=F32)  16.8 us
    dot_general x7, matrix products, mm_nt(): lax.dot_general(left, right, (((1,), (1,)), ((), ())), preferred_element_...  12.4 us

profile of v1, /device:TPU:8, one launch (start us, length us, event | category | flops | bytes accessed | tf_op | source)
XLA Modules:
  0.0 471.0 jit_solution(8389167189823124520)
XLA Ops:
  1.7 2.3 multiply_reduce_fusion.5
  5.9 70.6 %shard_map.212 = (bf16[2,4,4,2,16,1152]{5,4,3,2,1,0:T(8,128)(2,1)}, bf16[2,4,4,2,16,7296]{5,4,3,2,1,0:T(8,128)(2,1)}) custom-call(bf16[16,1152]{1,0:T(8,128)(2,1)} %concatenate.61.refs_0_, bf16[16,7296]{1,0:T(8,128)(2,1)} %fusion.48.refs_1_), custom_call_target="tpu_custom_call" | custom-call | tf_op jit(solution)/shard_map/pallas_call | solution.py:295
  76.5 1.2 slice_convert_fusion
  77.9 2.2 fusion.25
  80.7 1.2 fusion.55
  82.7 24.7 %shard_map.213.refs_0_ = bf16[2,4,4,1,256,128]{5,4,3,2,1,0:T(8,128)(2,1)} custom-call(bf16[256,128]{1,0:T(8,128)(2,1)} %maximum_bitcast_fusion.refs_0_), custom_call_target="tpu_custom_call" | custom-call | tf_op jit(solution)/shard_map/pallas_call | solution.py:295
  109.5 7.4 %shard_map.214 = bf16[64,896]{1,0:T(8,128)(2,1)} custom-call(bf16[64,896]{1,0:T(8,128)(2,1)} %bitcast.138), custom_call_target="tpu_custom_call" | custom-call | tf_op jit(solution)/shard_map/pallas_call | solution.py:342
  117.2 1.6 pad_maximum_fusion.2.refs_1_
  119.4 23.3 %shard_map.215 = (f32[2,64,896]{2,1,0:T(8,128)}, f32[2,1,896]{2,1,0:T(1,128)}) custom-call(bf16[2,4,4,1,256,128]{5,4,3,2,1,0:T(8,128)(2,1)} %shard_map.213.refs_0_, bf16[2,64,896]{2,1,0:T(8,128)(2,1)} %pad_maximum_fusion.2.refs_1_, s32[1,896]{1,0:T(1,128)} %bitcast.157), custom_call_target="tpu_custom_call" | custom-call | tf_op jit(solution)/shard_map/pallas_call | solution.py:524
  144.4 7.5 %shard_map.216 = bf16[64,896]{1,0:T(8,128)(2,1)} custom-call(bf16[64,896]{1,0:T(8,128)(2,1)} %get-tuple-element.96.refs_0_), custom_call_target="tpu_custom_call" | custom-call | tf_op jit(solution)/shard_map/pallas_call | solution.py:342
  153.1 2.6 convolution_convert_fusion.5.refs_0_
  155.8 15.9 %shard_map.217 = bf16[1024,256]{1,0:T(8,128)(2,1)} custom-call(bf16[1024,256]{1,0:T(8,128)(2,1)} %convolution_convert_fusion.5.refs_0_), custom_call_target="tpu_custom_call" | custom-call | tf_op jit(solution)/shard_map/pallas_call | solution.py:342
  171.7 1.4 multiply_reduce_fusion.4
  173.6 4.2 fusion.6
  178.6 4.2 fusion.8
  182.9 5.2 %multiply_convert_fusion.2 = (bf16[256,2432]{1,0:T(8,128)(2,1)S(1)}, bf16[256,2432]{1,0:T(8,128)(2,1)S(1)}, bf16[256,2432]{1,0:T(8,128)(2,1)S(1)}) fusion(f32[256,2432]{1,0:T(8,128)S(1)} %fusion.6, f32[256,2432]{1,0:T(8,128)S(1)} %fusion.8, bf16[1024,256]{1,0:T(8,128)(2,1)S(1)} %multiply_convert_fusion.3, bf16[1024,7296]{1,0:T(8,128)(2,1)} %bitcast.164), kind=kOutput, calls=%fused_computation.17 | convolution fusion | flops 1284407296 | bytes 14221312 | tf_op jit(solution)/shard_map/dot_general | solution.py:483
  188.2 1.5 fusion
  189.8 2.4 fusion.19.refs_0_
  192.1 2.3 fusion.16.refs_1_
  194.5 26.3 %shard_map.218 = (bf16[1024,256]{1,0:T(8,128)(2,1)}, bf16[1024,256]{1,0:T(8,128)(2,1)}) custom-call(bf16[1024,256]{1,0:T(8,128)(2,1)} %fusion.19.refs_0_, bf16[1024,256]{1,0:T(8,128)(2,1)} %fusion.16.refs_1_), custom_call_target="tpu_custom_call" | custom-call | tf_op jit(solution)/shard_map/pallas_call | solution.py:342
  220.8 2.8 fusion.22
  224.6 2.2 convolution_convert_fusion.10
  227.6 6.7 %shard_map.219 = bf16[64,896]{1,0:T(8,128)(2,1)} custom-call(bf16[64,896]{1,0:T(8,128)(2,1)} %bitcast.139), custom_call_target="tpu_custom_call" | custom-call | tf_op jit(solution)/shard_map/pallas_call | solution.py:342
  234.6 1.6 pad_maximum_fusion.4.refs_3_
  238.0 33.0 %shard_map.220 = (f32[2,64,896]{2,1,0:T(8,128)}, f32[2,4,4,1,256,128]{5,4,3,2,1,0:T(8,128)}) custom-call(bf16[2,4,4,1,256,128]{5,4,3,2,1,0:T(8,128)(2,1)} %shard_map.213.refs_0_, bf16[2,64,896]{2,1,0:T(8,128)(2,1)} %pad_maximum_fusion.2.refs_1_, s32[1,896]{1,0:T(1,128)} %bitcast.158, bf16[2,64,896]{2,1,0:T(8,128)(2,1)} %pad_maximum_fusion.4.refs_3_, ...), custom_call_target="tpu_custom_call" | custom-call | tf_op jit(solution)/shard_map/pallas_call | solution.py:524
  271.0 3.9 convert_element_type.174.part_ref
  274.9 25.8 %shard_map.222 = f32[256,128]{1,0:T(8,128)} custom-call(bf16[2,4,4,1,256,128]{5,4,3,2,1,0:T(8,128)(2,1)} %convert_element_type.174.part_ref), custom_call_target="tpu_custom_call" | custom-call | tf_op jit(solution)/shard_map/pallas_call | solution.py:317
  301.8 1.4 broadcast_multiply_fusion
  303.3 1.4 fusion.52
  305.6 7.6 %shard_map.221 = bf16[64,896]{1,0:T(8,128)(2,1)} custom-call(bf16[64,896]{1,0:T(8,128)(2,1)} %fusion.53.refs_0_), custom_call_target="tpu_custom_call" | custom-call | tf_op jit(solution)/shard_map/pallas_call | solution.py:342
  314.9 1.3 copy-done.23
  316.2 1.4 convolution_convert_fusion.6.refs_0_
  317.6 15.4 %shard_map.223 = bf16[1024,256]{1,0:T(8,128)(2,1)} custom-call(bf16[1024,256]{1,0:T(8,128)(2,1)} %convolution_convert_fusion.6.refs_0_), custom_call_target="tpu_custom_call" | custom-call | tf_op jit(solution)/shard_map/pallas_call | solution.py:342
  333.1 1.8 multiply_reduce_fusion.1
  334.9 2.7 fusion.23
  337.7 1.7 convolution_convert_fusion.3
  339.4 2.7 copy.122
  342.1 1.4 convolution_convert_fusion.4
  343.5 1.5 copy.123
  345.3 5.2 %convolution_convert_fusion.2 = bf16[1024,2432]{1,0:T(8,128)(2,1)} fusion(bf16[1024,256]{1,0:T(8,128)(2,1)S(1)} %copy-done.7, bf16[256,2432]{1,0:T(8,128)(2,1)} %copy-done.19), kind=kOutput, calls=%fused_computation.2 | convolution fusion | flops 1277558784 | bytes 6750208 | tf_op jit(solution)/shard_map/dot_general | solution.py:361
  350.5 3.8 convolution_convert_fusion.1
  354.4 3.8 convolution_convert_fusion
  358.1 28.9 %concatenate.76 = bf16[1024,8448]{1,0:T(8,128)(2,1)} concatenate(bf16[1024,576]{1,0:T(8,128)(2,1)S(1)} %copy-done.8, bf16[1024,448]{1,0:T(8,128)(2,1)S(1)} %copy.123, bf16[1024,128]{1,0:T(8,128)(2,1)S(1)} %pad.20, bf16[1024,2432]{1,0:T(8,128)(2,1)} %convolution_convert_fusion.2, bf16[1024,2432]{1,0:T(8,128)(2,1)} %convolution_convert_fusion.1, ...), dimensions={1} | concatenate | bytes 34603008 | tf_op jit(solution)/shard_map/concatenate | solution.py:646
  387.1 74.7 %shard_map.224 = f32[16,8448]{1,0:T(8,128)} custom-call(bf16[2,4,4,2,16,8448]{5,4,3,2,1,0:T(8,128)(2,1)} %bitcast.114), custom_call_target="tpu_custom_call" | custom-call | tf_op jit(solution)/shard_map/pallas_call | solution.py:317
  463.2 1.3 constant_dynamic-slice_fusion.1
  464.5 1.3 constant_dynamic-slice_fusion
  465.7 1.5 slice_reduce_fusion
  468.7 1.8 slice_bitcast_fusion
  (162 shorter events, 21.9 us)
Async XLA Ops:
  0.6 1.0 copy-start
  0.7 3.3 copy-start.30
  0.7 3.6 copy-start.27
  0.7 3.6 copy-start.28
  0.7 3.6 copy-start.32
  0.7 3.6 copy-start.33
  0.7 4.5 copy-start.24
  0.7 4.5 copy-start.25
  0.7 4.5 copy-start.26
  3.9 167.8 %copy-start.2 = (f32[1024,256]{1,0:T(8,128)}, f32[1024,256]{1,0:T(8,128)S(1)}, u32[]{:S(2)}) copy-start(f32[1024,256]{1,0:T(8,128)S(1)} %get-tuple-element.111) | copy-start | bytes 3145732
  3.9 74.0 %copy-start.34 = (pred[1024]{0:T(1024)(128)(4,1)S(1)}, pred[1024]{0:T(1024)(128)(4,1)}, u32[]{:S(2)}) copy-start(pred[1024]{0:T(1024)(128)(4,1)} %constant.77) | copy-start | bytes 3076
  77.7 2.5 copy-start.29
  153.1 20.0 %copy-start.20 = (bf16[7,64,128]{2,1,0:T(8,128)(2,1)}, bf16[7,64,128]{2,1,0:T(8,128)(2,1)S(1)}, u32[]{:S(2)}) copy-start(bf16[7,64,128]{2,1,0:T(8,128)(2,1)S(1)} %copy.110) | copy-start | bytes 344068
  173.6 9.3 %copy-start.6 = (bf16[1024,256]{1,0:T(8,128)(2,1)}, bf16[1024,256]{1,0:T(8,128)(2,1)S(1)}, u32[]{:S(2)}) copy-start(bf16[1024,256]{1,0:T(8,128)(2,1)S(1)} %multiply_convert_fusion.3) | copy-start | bytes 1572868
  173.6 4.2 copy-start.4
  173.6 4.2 copy-start.31
  178.6 45.6 %copy-start.11 = (bf16[1024,256]{1,0:T(8,128)(2,1)}, bf16[1024,256]{1,0:T(8,128)(2,1)S(1)}, u32[]{:S(2)}) copy-start(bf16[1024,256]{1,0:T(8,128)(2,1)S(1)} %convolution_convert_fusion.7) | copy-start | bytes 1572868
  178.6 9.5 %slice-start = ((s8[14942208]{0:T(1024)(128)(4,1)}), s8[4194304]{0:T(1024)(128)(4,1)S(1)}, s32[]{:S(2)}) async-start(s8[14942208]{0:T(1024)(128)(4,1)} %bitcast.165), calls=%async_computation | async-start | bytes 8388608
  178.6 9.5 %slice-start.1 = ((s8[14942208]{0:T(1024)(128)(4,1)}), s8[4194304]{0:T(1024)(128)(4,1)S(1)}, s32[]{:S(2)}) async-start(s8[14942208]{0:T(1024)(128)(4,1)} %bitcast.165), calls=%async_computation.1 | async-start | bytes 8388608
  182.8 5.3 %slice-start.2 = ((s8[14942208]{0:T(1024)(128)(4,1)}), s8[4194304]{0:T(1024)(128)(4,1)S(1)}, s32[]{:S(2)}) async-start(s8[14942208]{0:T(1024)(128)(4,1)} %bitcast.165), calls=%async_computation.2 | async-start | bytes 8388608
  182.9 5.3 %slice-start.3 = ((s8[14942208]{0:T(1024)(128)(4,1)}), s8[2359296]{0:T(1024)(128)(4,1)S(1)}, s32[]{:S(2)}) async-start(s8[14942208]{0:T(1024)(128)(4,1)} %bitcast.165), calls=%async_computation.3 | async-start | bytes 4718592
  188.1 1.6 copy-start.17
  188.1 1.6 copy-start.19
  188.1 4.0 copy-start.15
  220.8 2.8 copy-start.10
  220.8 2.8 copy-start.13
  224.6 11.6 %copy-start.14 = (f32[2,64,896]{2,1,0:T(8,128)S(1)}, f32[2,64,896]{2,1,0:T(8,128)}, u32[]{:S(2)}) copy-start(f32[2,64,896]{2,1,0:T(8,128)} %get-tuple-element.20) | copy-start | bytes 1376260
  274.9 30.0 %copy-start.22 = (f32[2,64,896]{2,1,0:T(8,128)S(1)}, f32[2,64,896]{2,1,0:T(8,128)}, u32[]{:S(2)}) copy-start(f32[2,64,896]{2,1,0:T(8,128)} %get-tuple-element.25) | copy-start | bytes 1376260
  314.5 1.7 copy-start.23
  316.2 16.9 %copy-start.3 = (f32[1024,256]{1,0:T(8,128)S(1)}, f32[1024,256]{1,0:T(8,128)}, u32[]{:S(2)}) copy-start(f32[1024,256]{1,0:T(8,128)} %copy-done.2) | copy-start | bytes 3145732
  317.6 17.3 %copy-start.9 = (bf16[1024,256]{1,0:T(8,128)(2,1)S(1)}, bf16[1024,256]{1,0:T(8,128)(2,1)}, u32[]{:S(2)}) copy-start(bf16[1024,256]{1,0:T(8,128)(2,1)} %convolution_convert_fusion.6.refs_0_) | copy-start | bytes 1572868
  333.1 1.9 copy-start.5
  337.7 4.4 copy-start.21
  342.1 3.2 copy-start.7
  345.3 5.2 %copy-start.18 = (bf16[256,2432]{1,0:T(8,128)(2,1)S(1)}, bf16[256,2432]{1,0:T(8,128)(2,1)}, u32[]{:S(2)}) copy-start(bf16[256,2432]{1,0:T(8,128)(2,1)} %copy-done.17) | copy-start | bytes 3735556
  350.5 3.8 copy-start.12
  350.5 3.8 copy-start.16
  354.4 3.8 copy-start.8
  387.1 83.5 %copy-start.1 = (bf16[1,256,896]{2,1,0:T(8,128)(2,1)S(1)}, bf16[1,256,896]{2,1,0:T(8,128)(2,1)}, u32[]{:S(2)}) copy-start(bf16[1,256,896]{2,1,0:T(8,128)(2,1)} %param.13) | copy-start | bytes 1376260

commit v2 on v1

v2 whole, which is shorter than its diff:
```python
import jax
import jax.numpy as jnp
import numpy as np
from jax import lax
from jax.experimental import pallas as pl
from jax.experimental.pallas import tpu as pltpu
from jax.sharding import PartitionSpec as P

MESH_ID = pl.DeviceIdType.MESH
ANY = pl.ANY
VMEM = pltpu.VMEM


class Place:
    def __init__(self):
        self.seq = lax.axis_index("seq")
        ctx = lax.axis_index("ctx")
        self.ctx = ctx
        self.tp = lax.axis_index("tp")
        self.core = ctx % 2
        core = self.core
        y, z = ctx // 8, (ctx // 2) % 4
        self.a = y * (1 - core) + z * core
        self.b = z * (1 - core) + y * core
        self.stride_a = 8 - 6 * core
        self.stride_b = 2 + 6 * core
        self.a_next = self.peer(1, 0)
        self.a_prev = self.peer(3, 0)
        self.b_next = self.peer(0, 1)
        self.b_prev = self.peer(0, 3)
        self.other_core = {"ctx": ctx + 1 - 2 * core}
        self.other_seq = {"seq": 1 - self.seq}
        self.mirror = {"ctx": 31 - ctx}
        self.other_tp = {"tp": 1 - self.tp}

    def peer(self, da, db):
        a, b = (self.a + da) % 4, (self.b + db) % 4
        return {"ctx": a * self.stride_a + b * self.stride_b + self.core}


def greet(peers):
    barrier = pltpu.get_barrier_semaphore()
    for peer in peers:
        pl.semaphore_signal(barrier, inc=1, device_id=peer, device_id_type=MESH_ID)
    pl.semaphore_wait(barrier, len(peers))


def remote(src, dst, send, recv, index, peer):
    return pltpu.make_async_remote_copy(
        src_ref=src,
        dst_ref=dst,
        send_sem=send.at[index],
        recv_sem=recv.at[index],
        device_id=peer,
        device_id_type=MESH_ID,
    )


GATHER_SEMS = 13


class Gather:
    def __init__(self, place, own, full, send, recv, local):
        self.p, self.own, self.full = place, own, full
        self.send, self.recv, self.local = send, recv, local
        self.pair = full.shape[3] == 2
        self.started = []

    def go(self, src, dst, index, peer):
        copy = remote(src, dst, self.send, self.recv, index, peer)
        copy.start()
        self.started.append(copy)

    def got(self, ref, index):
        remote(ref, ref, self.send, self.recv, index, self.p.a_next).wait_recv()

    def half(self, b, a, which):
        ref = self.full.at[self.p.core, b, a]
        if self.pair:
            return ref.at[which]
        rows = self.full.shape[4] // 2
        return ref.at[0, pl.ds(which * rows, rows)]

    def begin(self):
        p = self.p
        slot = self.full.at[p.core, p.b, p.a, p.seq if self.pair else 0]
        self.mine = pltpu.make_async_copy(self.own, slot, self.local)
        self.mine.start()
        if self.pair:
            self.go(self.own, slot, 0, p.other_seq)

    def first(self):
        p = self.p
        self.mine.wait()
        if self.pair:
            self.got(self.full.at[p.core, p.b, p.a, 1 - p.seq], 0)
        block = self.full.at[p.core, p.b, p.a]
        self.go(block, block, 1, p.a_next)
        self.go(block, block, 2, p.a_prev)

    def second(self):
        p = self.p
        down, up = (p.a + 3) % 4, (p.a + 1) % 4
        self.got(self.full.at[p.core, p.b, down], 1)
        half = self.half(p.b, down, 0)
        self.go(half, half, 3, p.a_next)
        self.got(self.full.at[p.core, p.b, up], 2)
        half = self.half(p.b, up, 1)
        self.go(half, half, 4, p.a_prev)

    def third(self):
        p = self.p
        far = (p.a + 2) % 4
        self.got(self.half(p.b, far, 0), 3)
        self.got(self.half(p.b, far, 1), 4)
        block = self.full.at[p.core, p.b]
        self.go(block, block, 5, p.b_next)
        self.go(block, block, 6, p.b_prev)
        self.go(block, block, 9, p.other_core)

    def fourth(self):
        p = self.p
        down, up = (p.b + 3) % 4, (p.b + 1) % 4
        block = self.full.at[p.core, down]
        self.got(block, 5)
        half = self.full.at[p.core, down, pl.ds(0, 2)]
        self.go(half, half, 7, p.b_next)
        self.go(block, block, 10, p.other_core)
        block = self.full.at[p.core, up]
        self.got(block, 6)
        half = self.full.at[p.core, up, pl.ds(2, 2)]
        self.go(half, half, 8, p.b_prev)
        self.go(block, block, 11, p.other_core)

    def fifth(self):
        p = self.p
        far = (p.b + 2) % 4
        self.got(self.full.at[p.core, far, pl.ds(0, 2)], 7)
        self.got(self.full.at[p.core, far, pl.ds(2, 2)], 8)
        block = self.full.at[p.core, far]
        self.go(block, block, 12, p.other_core)

    def finish(self):
        p = self.p
        for index, step in ((9, 0), (10, 3), (11, 1), (12, 2)):
            self.got(self.full.at[1 - p.core, (p.a + step) % 4], index)
        for copy in self.started:
            copy.wait_send()

    def peers(self):
        p = self.p
        found = [p.a_next, p.a_prev, p.b_next, p.b_prev, p.other_core]
        return found + ([p.other_seq] if self.pair else [])


def add_into(target, extra, count):
    def body(k, carry):
        total = target[k].astype(jnp.float32) + extra[k].astype(jnp.float32)
        target[k] = total.astype(target.dtype)
        return carry

    lax.fori_loop(0, count, body, 0)


SCATTER_SEMS = 13


class Scatter:
    @staticmethod
    def scratch(seqs, rows, width):
        bf16 = jnp.bfloat16
        return [
            VMEM((4, 4, seqs, rows, width), bf16),
            VMEM((2, 2, seqs, rows, width), bf16),
            VMEM((1, rows, width), bf16),
            pltpu.SemaphoreType.DMA((SCATTER_SEMS,)),
            pltpu.SemaphoreType.DMA((SCATTER_SEMS,)),
            pltpu.SemaphoreType.REGULAR,
        ]

    def __init__(self, place, part, scratch):
        self.p, self.part = place, part
        self.sums, self.far_b, self.across, self.send, self.recv, self.free = scratch
        self.seqs, self.rows = part.shape[3], part.shape[4]
        spare = part.at[1 - place.core]
        self.near_b = [spare.at[side] for side in range(2)]
        self.near_a = [spare.at[2, side] for side in range(2)]
        self.far_a = [spare.at[2, 2 + side, pl.ds(0, 1)] for side in range(2)]
        if self.seqs == 1:
            self.far_a = [ref.at[:, pl.ds(0, self.rows // 2)] for ref in self.far_a]
        self.started = []

    go = Gather.go
    got = Gather.got

    def half(self, b, a, which):
        ref = self.sums.at[b, a]
        if self.seqs == 2:
            return ref.at[pl.ds(which, 1)]
        rows = self.rows // 2
        return ref.at[:, pl.ds(which * rows, rows)]

    def begin(self):
        p = self.p
        for step in (2, 1, 3, 0):
            slot = (p.a + step) % 4
            self.go(self.part.at[1 - p.core, slot], self.sums.at[slot], step, p.other_core)

    def add_core(self, step):
        p = self.p
        slot = (p.b + step) % 4
        self.got(self.sums.at[slot], step)
        for a in range(4):
            add_into(self.sums.at[slot, a], self.part.at[p.core, slot, a], self.seqs)

    def first(self):
        p = self.p
        self.add_core(2)
        far = (p.b + 2) % 4
        self.go(self.sums.at[far, pl.ds(0, 2)], self.far_b.at[0], 4, p.b_next)
        self.go(self.sums.at[far, pl.ds(2, 2)], self.far_b.at[1], 5, p.b_prev)

    def second(self):
        p = self.p
        up, down = (p.b + 1) % 4, (p.b + 3) % 4
        for copy in self.started[:4]:
            copy.wait_send()
        self.started = self.started[4:]
        ring = (p.a_next, p.a_prev, p.b_next, p.b_prev)
        for peer in ring:
            pl.semaphore_signal(self.free, inc=1, device_id=peer, device_id_type=MESH_ID)
        self.add_core(1)
        self.add_core(3)
        pl.semaphore_wait(self.free, len(ring))
        self.got(self.far_b.at[0], 4)
        for a in range(2):
            add_into(self.sums.at[up, a], self.far_b.at[0, a], self.seqs)
        self.go(self.sums.at[up], self.near_b[0], 6, p.b_next)
        self.got(self.far_b.at[1], 5)
        for a in range(2):
            add_into(self.sums.at[down, a + 2], self.far_b.at[1, a], self.seqs)
        self.go(self.sums.at[down], self.near_b[1], 7, p.b_prev)
        self.add_core(0)

    def third(self):
        p = self.p
        for side in range(2):
            self.got(self.near_b[side], 6 + side)
            for a in range(4):
                add_into(self.sums.at[p.b, a], self.near_b[side].at[a], self.seqs)
        far = (p.a + 2) % 4
        self.go(self.half(p.b, far, 0), self.far_a[0], 8, p.a_next)
        self.go(self.half(p.b, far, 1), self.far_a[1], 9, p.a_prev)

    def fourth(self):
        p = self.p
        up, down = (p.a + 1) % 4, (p.a + 3) % 4
        self.got(self.far_a[0], 8)
        add_into(self.half(p.b, up, 0), self.far_a[0], 1)
        self.go(self.sums.at[p.b, up], self.near_a[0], 10, p.a_next)
        self.got(self.far_a[1], 9)
        add_into(self.half(p.b, down, 1), self.far_a[1], 1)
        self.go(self.sums.at[p.b, down], self.near_a[1], 11, p.a_prev)

    def fifth(self):
        p = self.p
        for side in range(2):
            self.got(self.near_a[side], 10 + side)
            add_into(self.sums.at[p.b, p.a], self.near_a[side], self.seqs)
        if self.seqs == 2:
            self.go(self.sums.at[p.b, p.a, pl.ds(1 - p.seq, 1)], self.across, 12, p.other_seq)

    def finish(self, out):
        p = self.p
        if self.seqs == 2:
            self.got(self.across, 12)
            out[...] = self.sums[p.b, p.a, p.seq].astype(jnp.float32) + self.across[0].astype(jnp.float32)
        else:
            out[...] = self.sums[p.b, p.a, 0].astype(jnp.float32)
        for copy in self.started:
            copy.wait_send()

    def peers(self):
        p = self.p
        found = [p.a_next, p.a_prev, p.b_next, p.b_prev, p.other_core]
        return found + ([p.other_seq] if self.seqs == 2 else [])


NEGATIVE = -1e30
HD = 64
ROWS = 896
TURNS = 33
F32, BF16 = jnp.float32, jnp.bfloat16


def mm(left, right):
    return jnp.dot(left, right, preferred_element_type=F32)


def mm_nt(left, right):
    return lax.dot_general(left, right, (((1,), (1,)), ((), ())), preferred_element_type=F32)


def slot_of(block):
    core, y, z = block % 2, block // 8, (block // 2) % 4
    a = y * (1 - core) + z * core
    b = z * (1 - core) + y * core
    return core, b, a


class Turn:
    def __init__(self, ctx, t, first):
        counts = (ctx + 1, 32 - ctx)
        inside = (t < counts[first]).astype(jnp.int32)
        self.segment = first * inside + (1 - first) * (1 - inside)
        self.block = t - counts[first] * (1 - inside)
        count = counts[0] * (1 - self.segment) + counts[1] * self.segment
        self.first_row = (count - 1) * 256 + 128 * self.segment
        self.hidden = (self.block == 0) | (self.block == count - 1)
        self.last = self.block == count - 1

    def scores(self, scores, doc_ref, hidden):
        if not hidden:
            return scores
        key = lax.broadcasted_iota(jnp.int32, (256, ROWS), 0) + self.block * 256
        row = lax.broadcasted_iota(jnp.int32, (256, ROWS), 1) % 128 + self.first_row
        visible = (key <= row) & (key >= doc_ref[self.segment])
        return jnp.where(visible, scores, NEGATIVE)


def run_turns(ctx, first, start, stop, step):
    def body(t, carry):
        turn = Turn(ctx, t, first)
        pl.when(turn.hidden)(lambda: step(turn, True))
        pl.when(jnp.logical_not(turn.hidden))(lambda: step(turn, False))
        return carry

    lax.fori_loop(start, stop, body, 0)


def attend_step(turn, hidden, kv_ref, q_ref, doc_ref, m_ref, l_ref, acc_ref):
    core, b, a = slot_of(turn.block)
    segment = turn.segment
    kv = kv_ref[core, b, a, 0]
    scores = turn.scores(mm(kv[:, :HD], q_ref[segment]), doc_ref, hidden)
    old = m_ref[segment]
    new = jnp.maximum(old, jnp.max(scores, 0, keepdims=True))
    probs = jnp.exp(scores - new)
    keep = jnp.exp(old - new)
    m_ref[segment] = new
    l_ref[segment] = l_ref[segment] * keep + jnp.sum(probs, 0, keepdims=True)
    acc_ref[segment] = acc_ref[segment] * keep + mm(kv[:, HD:].T, probs.astype(BF16))


def attend_back_step(turn, hidden, kv_ref, q_ref, doc_ref, do_ref, lse_ref, delta_ref, dq_ref, dkv_ref):
    core, b, a = slot_of(turn.block)
    segment = turn.segment
    kv = kv_ref[core, b, a, 0]
    keys, values = kv[:, :HD], kv[:, HD:]
    q, do = q_ref[segment], do_ref[segment]
    scores = turn.scores(mm(keys, q), doc_ref, hidden)
    probs = jnp.exp(scores - lse_ref[segment])
    dscores = (probs * (mm(values, do) - delta_ref[segment])).astype(BF16)
    dq_ref[segment] += mm(keys.T, dscores)
    dkv_ref[core, b, a, 0] += jnp.concatenate([mm_nt(dscores, q), mm_nt(probs.astype(BF16), do)], 1)


D, DPAD, FF_HERE, GROUP, GROUP_Q = 896, 1024, 2432, 576, 448
QKV_W, ATTN_W, FFN_W = 640, 1152, 3 * 2432
GAIN_ONE, GAIN_TWO = 576, 577
EPS_VALUE = 1e-06
THETA = 1000000.0
VMEM_BYTES = 62 << 20
CHUNK = 256


def slot_columns():
    index = np.arange(64)
    seq, y, z, core = index // 32, (index // 8) % 4, (index // 2) % 4, index % 2
    a, b = np.where(core == 0, y, z), np.where(core == 0, z, y)
    slot = ((core * 4 + b) * 4 + a) * 2 + seq
    columns = np.full((64, 16), -1)
    columns[slot, :14] = index[:, None] * 14 + np.arange(14)
    return columns.reshape(-1)


def mm_tn(left, right):
    return lax.dot_general(left, right, (((0,), (0,)), ((), ())), preferred_element_type=F32)


def rope_tables(positions):
    exponents = jnp.arange(HD // 2, dtype=F32) * (2.0 / HD)
    freqs = THETA ** (-exponents)
    angles = freqs[:, None] * positions.astype(F32)[None, :]
    angles = jnp.concatenate([angles, angles], 0)
    return jnp.cos(angles), jnp.sin(angles)


def rotate(values, cosine, sine):
    turned = jnp.concatenate([-values[32:], values[:32]], 0)
    return values * cosine + turned * sine


def rotate_back(grads, cosine, sine):
    sined = grads * sine
    return grads * cosine + jnp.concatenate([sined[32:], -sined[:32]], 0)


def inv_rms(values):
    return lax.rsqrt(jnp.sum(values * values, 0, keepdims=True) * (1.0 / D) + EPS_VALUE)


def norm_back(values, inverse, scaled):
    mean = jnp.sum(scaled * values, 0, keepdims=True) * (1.0 / D)
    return inverse * scaled - values * inverse**3 * mean


def head(index):
    return pl.ds(index * HD, HD)


def lanes(index):
    return pl.ds(index * 128, 128)


def flat(ref, start, width):
    return ref[:, :, :, :, :, pl.ds(start, width)].reshape(DPAD, width)


def unflat(value):
    return value.reshape(2, 4, 4, 2, 16, value.shape[-1])


def shape(dims, dtype):
    return jax.ShapeDtypeStruct(dims, dtype)


def forward_kernel(
    attn_row,
    ffn_row,
    x_in,
    ct_in,
    select,
    cosine,
    sine,
    doc,
    attn_full,
    ffn_full,
    x_out,
    ct_out,
    ct_tokens,
    normed_out,
    q_both,
    kv_full,
    attended,
    lse,
    att,
    middle,
    q_send,
    kv_mine,
    att_send,
    att_far,
    branch_send,
    branch_far,
    m_ref,
    l_ref,
    acc_ref,
    pair_send,
    pair_recv,
    *sems,
):
    p = Place()
    attn = Gather(p, attn_row, attn_full, *sems[0:3])
    ffn = Gather(p, ffn_row, ffn_full, *sems[3:6])
    keys = Gather(p, kv_mine, kv_full, *sems[6:9])
    greet(attn.peers() + [p.mirror, p.other_tp])
    attn.begin()
    ffn.begin()
    x = mm_nt(select[...], x_in[...])
    x_out[...] = x
    attn.first()
    ct_out[...] = mm_nt(select[...], ct_in[...]).astype(BF16)
    attn.second()
    ffn.first()
    ct_tokens[...] = mm_nt(ct_in[...], select[...]).astype(BF16)
    attn.third()
    attn.fourth()
    ffn.second()
    attn.fifth()
    attn.finish()
    ffn.third()

    gain = flat(attn_full, 512, 128)[:, GAIN_ONE - 512 : GAIN_ONE - 511].astype(F32)
    row = lax.broadcasted_iota(jnp.int32, (DPAD, 256), 0)
    x = x_out[...]
    normed = jnp.where(row % 16 == 14, 1.0, x * inv_rms(x) * gain)
    normed_out[...] = normed.astype(BF16)
    mixed = mm(normed.T.astype(BF16), flat(attn_full, 0, QKV_W)).T
    for h in range(7):
        query = rotate(mixed[64 * h : 64 * h + 64], cosine[...], sine[...]).astype(BF16).astype(F32) * 0.125
        q_both[0, :, lanes(h)] = query[:, :128].astype(BF16)
        q_send[:, lanes(h)] = query[:, 128:].astype(BF16)
    q_copy = remote(q_send, q_both.at[1], pair_send, pair_recv, 0, p.mirror)
    q_copy.start()
    key = rotate(mixed[GROUP_Q : GROUP_Q + HD], cosine[...], sine[...])
    kv_mine[...] = jnp.concatenate([key, mixed[GROUP_Q + HD : GROUP]], 0).T.astype(BF16)
    for stage in ("begin", "first", "second", "third", "fourth", "fifth", "finish"):
        getattr(keys, stage)()
    m_ref[...] = jnp.full(m_ref.shape, NEGATIVE, F32)
    l_ref[...] = jnp.zeros(l_ref.shape, F32)
    acc_ref[...] = jnp.zeros(acc_ref.shape, F32)
    q_copy.wait()
    ffn.fourth()

    def step(turn, hidden):
        attend_step(turn, hidden, kv_full, q_both, doc, m_ref, l_ref, acc_ref)

    run_turns(p.ctx, 1, 0, 16, step)
    ffn.fifth()
    run_turns(p.ctx, 1, 16, TURNS, step)
    attended[...] = acc_ref[...] / l_ref[...]
    att_send[...] = attended[1].astype(BF16)
    att_copy = remote(att_send, att_far, pair_send, pair_recv, 1, p.mirror)
    att_copy.start()
    lse[...] = m_ref[...] + jnp.log(l_ref[...])
    att[pl.ds(GROUP_Q, 64), :] = jnp.zeros((64, 256), BF16)
    for h in range(7):
        att[head(h), lanes(0)] = attended[0, :, lanes(h)].astype(BF16)
    att_copy.wait()
    for h in range(7):
        att[head(h), lanes(1)] = att_far[:, lanes(h)]
    branch_send[...] = mm(flat(attn_full, QKV_W, 512), att[...]).astype(BF16)
    branch_copy = remote(branch_send, branch_far, pair_send, pair_recv, 2, p.other_tp)
    branch_copy.start()
    ffn.finish()
    branch_copy.wait()
    middle[...] = x_out[...] + (branch_send[...].astype(F32) + branch_far[...].astype(F32))


def forward(attn_row, ffn_row, x, ct, select, cosine, sine, doc):
    dma = pltpu.SemaphoreType.DMA
    gather_sems = [dma((GATHER_SEMS,)), dma((GATHER_SEMS,)), dma]
    in_vmem, in_hbm = pl.BlockSpec(memory_space=VMEM), pl.BlockSpec(memory_space=ANY)
    return pl.pallas_call(
        forward_kernel,
        out_shape=[
            shape((2, 4, 4, 2, 16, ATTN_W), BF16),
            shape((2, 4, 4, 2, 16, FFN_W), BF16),
            shape((DPAD, 256), F32),
            shape((DPAD, 256), BF16),
            shape((256, DPAD), BF16),
            shape((DPAD, 256), BF16),
            shape((2, HD, ROWS), BF16),
            shape((2, 4, 4, 1, 256, 128), BF16),
            shape((2, HD, ROWS), F32),
            shape((2, 1, ROWS), F32),
            shape((512, 256), BF16),
            shape((DPAD, 256), F32),
        ],
        in_specs=[in_vmem, in_hbm] + [in_vmem] * 6,
        out_specs=[in_vmem, in_hbm] + [in_vmem] * 10,
        scratch_shapes=[
            VMEM((HD, ROWS), BF16),
            VMEM((256, 128), BF16),
            VMEM((HD, ROWS), BF16),
            VMEM((HD, ROWS), BF16),
            VMEM((DPAD, 256), BF16),
            VMEM((DPAD, 256), BF16),
            VMEM((2, 1, ROWS), F32),
            VMEM((2, 1, ROWS), F32),
            VMEM((2, HD, ROWS), F32),
            dma((3,)),
            dma((3,)),
        ]
        + gather_sems * 3,
        compiler_params=pltpu.CompilerParams(collective_id=0, has_side_effects=True, vmem_limit_bytes=VMEM_BYTES),
    )(attn_row, ffn_row, x, ct, select, cosine, sine, doc)


def ffn_chunk(weights, slot, width, normed, tokens, ct, ct_tokens, part, start, out_sum, grad_sum):
    w_gate, w_up, w_down = (weights[slot, k, :, pl.ds(0, width)] for k in range(3))
    gate, up = mm(tokens[...], w_gate), mm(tokens[...], w_up)
    grad_hidden = mm(ct_tokens[...], w_down)
    sigmoid = jax.nn.sigmoid(gate)
    silu = gate * sigmoid
    hidden = (silu * up).astype(BF16)
    grad_up = (grad_hidden * silu).astype(BF16)
    grad_gate = (grad_hidden * up * sigmoid * (1.0 + gate * (1.0 - sigmoid))).astype(BF16)
    grad_sum[...] += mm_nt(w_gate, grad_gate) + mm_nt(w_up, grad_up)
    out_sum[...] += mm_nt(w_down, hidden)
    for k, (left, right) in enumerate(((normed, grad_gate), (normed, grad_up), (ct, hidden))):
        part[:, :, :, :, :, pl.ds(k * FF_HERE + start, width)] = unflat(mm(left[...], right).astype(BF16))


def backward_kernel(
    attn_full,
    ffn_full,
    x_kept,
    ct,
    ct_tokens,
    normed_kept,
    q_both,
    kv_full,
    attended,
    lse,
    att,
    middle,
    cosine,
    sine,
    doc,
    output,
    grad_inputs,
    attn_mine,
    ffn_mine,
    weights,
    normed_ffn,
    tokens,
    out_sum,
    grad_sum,
    out_far,
    grad_far,
    do_both,
    delta,
    dq,
    dq_send,
    dq_far,
    dkv,
    kv_part,
    kv_mine,
    grad_mixed,
    ffn_part,
    attn_part,
    gains_far,
    grad_free,
    weight_sems,
    kept_sems,
    pair_send,
    pair_recv,
    *scratch,
):
    p = Place()
    out_send, grad_send, do_send = output, grad_inputs, dq_send
    ffn = Scatter(p, ffn_part, scratch[0:6])
    keys = Scatter(p, kv_part, scratch[6:12])
    attn = Scatter(p, attn_part, scratch[12:18])

    def load(index, slot, width):
        start = index * CHUNK
        copies = []
        for k in range(3):
            place = pl.ds(pl.multiple_of(k * FF_HERE + start, 128), width)
            copies.append(
                pltpu.make_async_copy(
                    ffn_full.at[:, place], weights.at[slot, k, :, pl.ds(0, width)], weight_sems.at[slot, k]
                )
            )
        return copies

    for copy in load(0, 0, CHUNK):
        copy.start()
    greet(ffn.peers() + [p.mirror, p.other_tp])
    gain_two = flat(attn_full, 512, 128)[:, GAIN_TWO - 512 : GAIN_TWO - 511].astype(F32)
    mid = middle[...]
    inverse = inv_rms(mid)
    scaled = mid * inverse * gain_two
    normed_ffn[...] = scaled.astype(BF16)
    tokens[...] = scaled.T.astype(BF16)
    out_sum[...] = jnp.zeros(out_sum.shape, F32)
    grad_sum[...] = jnp.zeros(grad_sum.shape, F32)
    chunks, tail = FF_HERE // CHUNK, FF_HERE % CHUNK

    def chunk_body(index, carry):
        slot = index % 2
        for copy in load(index, slot, CHUNK):
            copy.wait()

        @pl.when(index < chunks - 1)
        def _():
            for copy in load(index + 1, 1 - slot, CHUNK):
                copy.start()

        @pl.when(index == chunks - 1)
        def _():
            for copy in load(chunks, chunks % 2, tail):
                copy.start()

        start = pl.multiple_of(index * CHUNK, 128)
        ffn_chunk(weights, slot, CHUNK, normed_ffn, tokens, ct, ct_tokens, ffn_part, start, out_sum, grad_sum)
        return carry

    lax.fori_loop(0, chunks, chunk_body, 0)
    for copy in load(chunks, chunks % 2, tail):
        copy.wait()
    ffn_chunk(
        weights, chunks % 2, tail, normed_ffn, tokens, ct, ct_tokens, ffn_part, chunks * CHUNK, out_sum, grad_sum
    )
    grad_send[...] = grad_sum[...].astype(BF16)
    grad_copy = remote(grad_send, grad_far, pair_send, pair_recv, 0, p.other_tp)
    grad_copy.start()
    ffn.begin()
    out_send[...] = out_sum[...].astype(BF16)
    out_copy = remote(out_send, out_far, pair_send, pair_recv, 1, p.other_tp)
    out_copy.start()
    x, normed, grad_middle = out_sum, normed_ffn, grad_sum
    kept = [
        pltpu.make_async_copy(x_kept, x, kept_sems.at[0]),
        pltpu.make_async_copy(normed_kept, normed, kept_sems.at[1]),
    ]
    for copy in kept:
        copy.start()
    dq[...] = jnp.zeros(dq.shape, F32)
    dkv[...] = jnp.zeros(dkv.shape, F32)
    grad_copy.wait()
    mid = middle[...]
    inverse = inv_rms(mid)
    grad_normed = grad_send[...].astype(F32) + grad_far[...].astype(F32)
    pl.semaphore_signal(grad_free, inc=1, device_id=p.other_tp, device_id_type=MESH_ID)
    gain_two_grad = jnp.sum(grad_normed * mid * inverse, 1, keepdims=True)
    grad_mid = ct[...].astype(F32) + norm_back(mid, inverse, grad_normed * gain_two)
    grad_middle[...] = grad_mid
    w_out = flat(attn_full, QKV_W, 512)
    grad_att = mm(grad_mid.T.astype(BF16), w_out).T
    for h in range(7):
        do_both[0, :, lanes(h)] = grad_att[64 * h : 64 * h + 64, :128].astype(BF16)
        do_send[:, lanes(h)] = grad_att[64 * h : 64 * h + 64, 128:].astype(BF16)
    do_copy = remote(do_send, do_both.at[1], pair_send, pair_recv, 2, p.mirror)
    do_copy.start()
    ffn.first()
    do_copy.wait()
    delta[...] = jnp.sum(do_both[...].astype(F32) * attended[...], 1, keepdims=True)

    def step(turn, hidden):
        attend_back_step(turn, hidden, kv_full, q_both, doc, do_both, lse, delta, dq, dkv)

    run_turns(p.ctx, 0, 0, 10, step)
    ffn.second()
    run_turns(p.ctx, 0, 10, TURNS, step)
    dq_send[...] = dq[1].astype(BF16)
    dq_copy = remote(dq_send, dq_far, pair_send, pair_recv, 3, p.mirror)
    dq_copy.start()
    kv_part[...] = dkv[...].astype(BF16)
    keys.begin()
    ffn.third()
    keys.first()
    out_copy.wait()
    output[...] = (middle[...] + (out_send[...].astype(F32) + out_far[...].astype(F32))).astype(BF16)
    keys.second()
    attn_part[:, :, :, :, :, pl.ds(QKV_W, 512)] = unflat(mm_nt(grad_middle[...].astype(BF16), att[...]).astype(BF16))
    keys.third()
    ffn.fourth()
    keys.fourth()
    keys.fifth()
    keys.finish(kv_mine)
    ffn.fifth()
    dq_copy.wait()
    grad_mixed[pl.ds(GROUP, QKV_W - GROUP), :] = jnp.zeros((QKV_W - GROUP, 256), BF16)
    for h in range(7):
        far = dq_far[:, lanes(h)].astype(F32)
        near = dq[0, :, lanes(h)]
        grad_query = jnp.concatenate([near, far], 1) * 0.125
        grad_mixed[head(h), :] = rotate_back(grad_query, cosine[...], sine[...]).astype(BF16)
    grad_kv = kv_mine[...].T
    grad_mixed[head(7), :] = rotate_back(grad_kv[:HD], cosine[...], sine[...]).astype(BF16)
    grad_mixed[head(8), :] = grad_kv[HD:].astype(BF16)
    w_qkv = flat(attn_full, 0, QKV_W)
    grad_normed = mm(w_qkv, grad_mixed[...])
    grad_send[...] = grad_normed.astype(BF16)
    pl.semaphore_wait(grad_free, 1)
    grad_copy = remote(grad_send, grad_far, pair_send, pair_recv, 4, p.other_tp)
    grad_copy.start()
    for copy in kept:
        copy.wait()
    value = x[...]
    inverse = inv_rms(value)
    gain_one_grad = jnp.sum(grad_normed * value * inverse, 1, keepdims=True)
    grad_qkv = mm_nt(normed[...], grad_mixed[...])
    lane = lax.broadcasted_iota(jnp.int32, grad_qkv.shape, 1)
    grad_qkv = jnp.where(lane == GAIN_ONE, gain_one_grad, jnp.where(lane == GAIN_TWO, gain_two_grad, grad_qkv))
    attn_part[:, :, :, :, :, pl.ds(0, QKV_W)] = unflat(grad_qkv.astype(BF16))
    attn.begin()
    ffn.finish(ffn_mine)
    attn.first()
    attn.second()
    grad_copy.wait()
    gain_one = flat(attn_full, 512, 128)[:, GAIN_ONE - 512 : GAIN_ONE - 511].astype(F32)
    scaled = (grad_send[...].astype(F32) + grad_far[...].astype(F32)) * gain_one
    grad_inputs[...] = (grad_middle[...] + norm_back(value, inverse, scaled)).astype(BF16)
    attn.third()
    attn.fourth()
    attn.fifth()
    attn.finish(attn_mine)
    gains_copy = remote(attn_mine.at[:, pl.ds(512, 128)], gains_far, pair_send, pair_recv, 5, p.other_tp)
    gains_copy.start()
    gains_copy.wait()
    mine = attn_mine[:, pl.ds(512, 128)]
    lane = lax.broadcasted_iota(jnp.int32, (16, 128), 1) + 512
    attn_mine[:, pl.ds(512, 128)] = mine + jnp.where(lane == GAIN_ONE, gains_far[...], 0.0)


def backward(*arrays):
    dma = pltpu.SemaphoreType.DMA
    in_vmem, in_hbm = pl.BlockSpec(memory_space=VMEM), pl.BlockSpec(memory_space=ANY)
    wide, tall, low = (DPAD, 256), (256, DPAD), (2, HD, ROWS)
    return pl.pallas_call(
        backward_kernel,
        out_shape=[shape(wide, BF16), shape(wide, BF16), shape((16, ATTN_W), F32), shape((16, FFN_W), F32)],
        in_specs=[in_vmem, in_hbm, in_hbm, in_vmem, in_vmem, in_hbm] + [in_vmem] * 9,
        out_specs=[in_vmem] * 4,
        scratch_shapes=[
            VMEM((2, 3, DPAD, CHUNK), BF16),
            VMEM(wide, BF16),
            VMEM(tall, BF16),
            VMEM(wide, F32),
            VMEM(wide, F32),
            VMEM(wide, BF16),
            VMEM(wide, BF16),
            VMEM(low, BF16),
            VMEM((2, 1, ROWS), F32),
            VMEM(low, F32),
            VMEM((HD, ROWS), BF16),
            VMEM((HD, ROWS), BF16),
            VMEM((2, 4, 4, 1, 256, 128), F32),
            VMEM((2, 4, 4, 1, 256, 128), BF16),
            VMEM((256, 128), F32),
            VMEM((QKV_W, 256), BF16),
            VMEM((2, 4, 4, 2, 16, FFN_W), BF16),
            VMEM((2, 4, 4, 2, 16, ATTN_W), BF16),
            VMEM((16, 128), F32),
            pltpu.SemaphoreType.REGULAR,
            dma((2, 3)),
            dma((2,)),
            dma((6,)),
            dma((6,)),
        ]
        + Scatter.scratch(2, 16, FFN_W)
        + Scatter.scratch(1, 256, 128)
        + Scatter.scratch(2, 16, ATTN_W),
        compiler_params=pltpu.CompilerParams(collective_id=1, has_side_effects=True, vmem_limit_bytes=VMEM_BYTES),
    )(*arrays)


def shards(
    inputs,
    positions,
    query_key_value_weight,
    query_key_value_bias,
    gain_attn,
    output_weight,
    gate_weight,
    up_weight,
    down_weight,
    gain_ffn,
    cotangent,
):
    me = lax.axis_index("seq") * 32 + lax.axis_index("ctx")
    select = jnp.asarray(slot_columns()[:, None] == np.arange(D)[None, :], BF16)
    bias_row = lax.dynamic_update_slice(jnp.zeros((1, GROUP), BF16), query_key_value_bias, (0, 9 * me))
    attn_row = jnp.concatenate(
        [
            jnp.concatenate([query_key_value_weight[:, 0], bias_row, jnp.zeros((1, GROUP), BF16)], 0),
            jnp.pad(jnp.stack([gain_attn, gain_ffn], 1), ((0, 2), (0, 62))),
            jnp.pad(output_weight[0].T, ((0, 2), (0, 64))),
        ],
        1,
    )
    ffn_row = jnp.pad(jnp.concatenate([gate_weight, up_weight, down_weight.T], 1), ((0, 2), (0, 0)))
    cosine, sine = rope_tables(positions[0])
    row = lax.axis_index("ctx") * 256 + jnp.arange(128, dtype=jnp.int32)
    doc = jnp.stack([jnp.tile((row - positions[0, :128])[None], (1, 7)), jnp.full((1, ROWS), 128, jnp.int32)])
    attn_full, ffn_full, *kept = forward(
        attn_row, ffn_row, inputs[0], cotangent[0], select, cosine, sine, doc
    )
    output, grad_inputs, attn, ffn = backward(
        attn_full, ffn_full.reshape(DPAD, FFN_W), *kept, cosine, sine, doc
    )
    return (
        mm_tn(output, select).astype(BF16)[None],
        mm_tn(grad_inputs, select).astype(BF16)[None],
        attn[:14, None, :GROUP],
        lax.dynamic_slice(attn, (14, 8 * me), (1, 8)),
        lax.dynamic_slice(attn, (14, 512 + me), (1, 1)),
        attn[:14, GAIN_ONE],
        attn[:14, QKV_W : QKV_W + GROUP_Q].T[None],
        ffn[:14, :FF_HERE],
        ffn[:14, FF_HERE : 2 * FF_HERE],
        ffn[:14, 2 * FF_HERE :].T,
        attn[:14, GAIN_TWO],
    )


def solution(mesh):
    both = ("seq", "ctx")
    return jax.shard_map(
        shards,
        mesh=mesh,
        in_specs=(
            P("seq", "ctx", None),
            P("seq", "ctx"),
            P(both, "tp", None),
            P("tp", both),
            P(both),
            P("tp", None, both),
            P(both, "tp"),
            P(both, "tp"),
            P("tp", both),
            P(both),
            P("seq", "ctx", None),
        ),
        out_specs=(
            P("seq", "ctx", None),
            P("seq", "ctx", None),
            P(both, "tp", None),
            P("tp", both),
            P("tp", both),
            P(both),
            P("tp", None, both),
            P(both, "tp"),
            P(both, "tp"),
            P("tp", both),
            P(both),
        ),
        check_vma=False,
    )
```

time: 479 us -> 273 us (0.57); the launches traced: 471 us -> 271 us
  Pallas kernels: 339 us -> 253 us
  matrix products: 52.9 us -> 4.04 us
  local copies, waits for them, and re-layouts: 56 us -> 8.13 us
  other arithmetic: 21 us -> 5.34 us
    pallas_call x13 -> x2, Pallas kernels: 339 us -> 253 us  [the longest x1 137 us: backward(): pl.pallas_call(backward_kernel, out_shape=[shape(wide, BF16), shape(wide,...]
    dot_general x12 -> x0, matrix products: 29.3 us -> none  [the longest x5 16.8 us: mm(): return jnp.dot(left, right, preferred_element_type=F32)]
    concatenate x3 -> x0, local copies, waits for them, and re-layouts: 29.3 us -> none  [the longest x1 28.9 us: shards(): jnp.concatenate([grad_qkv.astype(BF16), grad_out_w.astype(BF16), jnp.pad(...]
    dot_general x7 -> x2, matrix products: 23.6 us -> 4.04 us  [mm_tn(): lax.dot_general(left, right, (((0,), (0,)), ((), ())), preferred_element_...]
    convert_element_type x5 -> x0, local copies, waits for them, and re-layouts: 5.87 us -> none  [the longest x1 2.66 us: shards(): grad_qkv.astype(BF16)]
    convert_element_type x3 -> x0, other arithmetic: 5.16 us -> none  [the longest x1 3.9 us: shards(): grad_kv = scatter_sum(grad_kv.astype(BF16), 8).T]
    unnamed x90 -> x8, local copies, waits for them, and re-layouts: 6.4 us -> 1.31 us
    reduce_sum x4 -> x0, other arithmetic: 4.82 us -> none  [the longest x2 2.41 us: norm_back(): grad_gain = jnp.sum(grad_normed * values * inv_rms, 1, keepdims=True)]
where the time goes in v2:
time: 273 us; the launch traced here: 271 us
  Pallas kernels  253 us (93%)
  local copies, waits for them, and re-layouts  8.13 us (3%)
  other arithmetic  5.34 us (2%)
  matrix products  4.04 us (1%)
    pallas_call x1, Pallas kernels, backward(): pl.pallas_call(backward_kernel, out_shape=[shape(wide, BF16), shape(wide,...  137 us
    pallas_call x1, Pallas kernels, forward(): pl.pallas_call(forward_kernel, out_shape=[shape((2, 4, 4, 2, 16, ATTN_W),...  116 us

profile of v2, /device:TPU:8, one launch (start us, length us, event | category | flops | bytes accessed | tf_op | source)
XLA Modules:
  0.0 271.4 jit_solution(848807603479512345)
XLA Ops:
  0.7 0.9 dynamic_update_slice.3
  1.5 0.7 pad_maximum_fusion.1
  2.3 0.7 pad.14
  3.0 0.7 pad_maximum_fusion.2
  3.7 0.1 copy.31
  3.8 0.7 concatenate.13.attn_row
  4.5 0.7 bitcast_subtract_fusion
  5.2 0.6 stack.15.doc
  5.8 0.7 convert_element_type.16
  6.5 0.1 broadcast_multiply_fusion
  6.6 0.8 fusion.7
  7.4 1.7 fusion.6.ffn_row
  9.1 116.5 %shard_map.203 = (bf16[2,4,4,2,16,1152]{5,4,3,2,1,0:T(8,128)(2,1)}, bf16[2,4,4,2,16,7296]{5,4,3,2,1,0:T(8,128)(2,1)}, f32[1024,256]{1,0:T(8,128)}, bf16[1024,256...) custom-call(bf16[16,1152]{1,0:T(8,128)(2,1)} %concatenate.13.attn_ro, ...), custom_call_target="tpu_custom_call" | custom-call | tf_op jit(solution)/shard_map/pallas_call | solution.py:544
  125.5 0.0 copy-start
  125.6 136.7 %shard_map.204 = (bf16[1024,256]{1,0:T(8,128)(2,1)}, bf16[1024,256]{1,0:T(8,128)(2,1)}, f32[16,1152]{1,0:T(8,128)}, f32[16,7296]{1,0:T(8,128)}) custom-call(bf16[2,4,4,2,16,1152]{5,4,3,2,1,0:T(8,128)(2,1)} %get-tuple-element.27.attn_full, bf16[1024,7296]{1,0:T(8,128)(2,1)} %bitcast.29, f32[1024,256]{1,0:T(8,128)} %get-tuple-element.29.x_kept, ...), custom_call_target="tpu_custom_call" | custom-call | tf_op jit(solution)/shard_map/pallas_call | solution.py:804
  262.3 0.0 copy-start.1
  262.3 1.9 slice_bitcast_fusion
  264.2 0.0 copy-done
  264.2 2.5 fusion
  266.7 0.0 copy-start.2
  266.7 0.0 copy-done.1
  266.7 1.5 fusion.1
  268.2 0.0 copy-done.2
  268.3 0.7 copy.32
  268.9 0.6 copy.33
  269.6 0.6 constant_dynamic-slice_fusion.1
  270.1 0.6 constant_dynamic-slice_fusion
  270.7 0.7 slice_reduce_fusion
  (8 shorter events, 0.1 us)
Async XLA Ops:
  125.5 138.7 %copy-start = (bf16[1024,896]{1,0:T(8,128)(2,1)S(1)}, bf16[1024,896]{1,0:T(8,128)(2,1)}, u32[]{:S(2)}) copy-start(bf16[1024,896]{1,0:T(8,128)(2,1)} %constant.41.clone.select) | copy-start | bytes 5505028
  262.3 4.5 %copy-start.1 = (bf16[1024,256]{1,0:T(8,128)(2,1)S(1)}, bf16[1024,256]{1,0:T(8,128)(2,1)}, u32[]{:S(2)}) copy-start(bf16[1024,256]{1,0:T(8,128)(2,1)} %get-tuple-element.40) | copy-start | bytes 1572868
  266.7 1.5 copy-start.2

commit v3 on v2

--- a/solution.py
+++ b/solution.py
@@ -32,6 +32,7 @@
         self.other_seq = {"seq": 1 - self.seq}
         self.mirror = {"ctx": 31 - ctx}
         self.other_tp = {"tp": 1 - self.tp}
+        self.mirror_tp = {"ctx": 31 - ctx, "tp": 1 - self.tp}
 
     def peer(self, da, db):
         a, b = (self.a + da) % 4, (self.b + db) % 4
@@ -56,7 +57,7 @@
     )
 
 
-GATHER_SEMS = 13
+GATHER_SEMS = 15
 
 
 class Gather:
@@ -108,29 +109,48 @@
         half = self.half(p.b, up, 1)
         self.go(half, half, 4, p.a_prev)
 
-    def third(self):
+    def third_near(self):
         p = self.p
         far = (p.a + 2) % 4
         self.got(self.half(p.b, far, 0), 3)
         self.got(self.half(p.b, far, 1), 4)
-        block = self.full.at[p.core, p.b]
-        self.go(block, block, 5, p.b_next)
-        self.go(block, block, 6, p.b_prev)
-        self.go(block, block, 9, p.other_core)
+        row = self.full.at[p.core, p.b]
+        self.go(row.at[pl.ds(0, 2)], row.at[pl.ds(0, 2)], 5, p.b_next)
+        self.go(row.at[pl.ds(2, 2)], row.at[pl.ds(2, 2)], 6, p.b_prev)
+        self.go(row, row, 9, p.other_core)
+
+    def third_rest(self):
+        p = self.p
+        row = self.full.at[p.core, p.b]
+        self.go(row.at[pl.ds(2, 2)], row.at[pl.ds(2, 2)], 13, p.b_next)
+        self.go(row.at[pl.ds(0, 2)], row.at[pl.ds(0, 2)], 14, p.b_prev)
+
+    def third(self):
+        self.third_near()
+        self.third_rest()
+
+    def fourth_near(self):
+        p = self.p
+        half = self.full.at[p.core, (p.b + 3) % 4, pl.ds(0, 2)]
+        self.got(half, 5)
+        self.go(half, half, 7, p.b_next)
+        half = self.full.at[p.core, (p.b + 1) % 4, pl.ds(2, 2)]
+        self.got(half, 6)
+        self.go(half, half, 8, p.b_prev)
+
+    def fourth_rest(self):
+        p = self.p
+        down, up = (p.b + 3) % 4, (p.b + 1) % 4
+        self.got(self.full.at[p.core, down, pl.ds(2, 2)], 13)
+        row = self.full.at[p.core, down]
+        self.go(row, row, 10, p.other_core)
+        self.got(self.full.at[p.core, up, pl.ds(0, 2)], 14)
+        row = self.full.at[p.core, up]
+        self.go(row, row, 11, p.other_core)
 
     def fourth(self):
-        p = self.p
-        down, up = (p.b + 3) % 4, (p.b + 1) % 4
-        block = self.full.at[p.core, down]
-        self.got(block, 5)
-        half = self.full.at[p.core, down, pl.ds(0, 2)]
-        self.go(half, half, 7, p.b_next)
-        self.go(block, block, 10, p.other_core)
-        block = self.full.at[p.core, up]
-        self.got(block, 6)
-        half = self.full.at[p.core, up, pl.ds(2, 2)]
-        self.go(half, half, 8, p.b_prev)
-        self.go(block, block, 11, p.other_core)
+        self.fourth_near()
+        self.fourth_rest()
 
     def fifth(self):
         p = self.p
@@ -141,9 +161,15 @@
         self.go(block, block, 12, p.other_core)
 
     def finish(self):
-        p = self.p
-        for index, step in ((9, 0), (10, 3), (11, 1), (12, 2)):
-            self.got(self.full.at[1 - p.core, (p.a + step) % 4], index)
+        for step in (0, 3, 1, 2):
+            self.from_core(step)
+        self.sent()
+
+    def from_core(self, step):
+        p = self.p
+        self.got(self.full.at[1 - p.core, (p.a + step) % 4], {0: 9, 3: 10, 1: 11, 2: 12}[step])
+
+    def sent(self):
         for copy in self.started:
             copy.wait_send()
 
@@ -200,11 +226,14 @@
         rows = self.rows // 2
         return ref.at[:, pl.ds(which * rows, rows)]
 
+    def to_core(self, step):
+        p = self.p
+        slot = (p.a + step) % 4
+        self.go(self.part.at[1 - p.core, slot], self.sums.at[slot], step, p.other_core)
+
     def begin(self):
-        p = self.p
         for step in (2, 1, 3, 0):
-            slot = (p.a + step) % 4
-            self.go(self.part.at[1 - p.core, slot], self.sums.at[slot], step, p.other_core)
+            self.to_core(step)
 
     def add_core(self, step):
         p = self.p
@@ -240,10 +269,10 @@
         for a in range(2):
             add_into(self.sums.at[down, a + 2], self.far_b.at[1, a], self.seqs)
         self.go(self.sums.at[down], self.near_b[1], 7, p.b_prev)
+
+    def third(self):
+        p = self.p
         self.add_core(0)
-
-    def third(self):
-        p = self.p
         for side in range(2):
             self.got(self.near_b[side], 6 + side)
             for a in range(4):
@@ -301,23 +330,20 @@
     return lax.dot_general(left, right, (((1,), (1,)), ((), ())), preferred_element_type=F32)
 
 
-def slot_of(block):
-    core, y, z = block % 2, block // 8, (block // 2) % 4
-    a = y * (1 - core) + z * core
-    b = z * (1 - core) + y * core
-    return core, b, a
+def block_of(core, b, a):
+    y = a * (1 - core) + b * core
+    z = b * (1 - core) + a * core
+    return y * 8 + z * 2 + core
 
 
 class Turn:
-    def __init__(self, ctx, t, first):
-        counts = (ctx + 1, 32 - ctx)
-        inside = (t < counts[first]).astype(jnp.int32)
-        self.segment = first * inside + (1 - first) * (1 - inside)
-        self.block = t - counts[first] * (1 - inside)
-        count = counts[0] * (1 - self.segment) + counts[1] * self.segment
-        self.first_row = (count - 1) * 256 + 128 * self.segment
+    def __init__(self, ctx, segment, slot):
+        self.segment, self.slot = segment, slot
+        self.block = block_of(*slot)
+        count = (ctx + 1) * (1 - segment) + (32 - ctx) * segment
+        self.first_row = (count - 1) * 256 + 128 * segment
+        self.needed = self.block < count
         self.hidden = (self.block == 0) | (self.block == count - 1)
-        self.last = self.block == count - 1
 
     def scores(self, scores, doc_ref, hidden):
         if not hidden:
@@ -328,18 +354,18 @@
         return jnp.where(visible, scores, NEGATIVE)
 
 
-def run_turns(ctx, first, start, stop, step):
-    def body(t, carry):
-        turn = Turn(ctx, t, first)
-        pl.when(turn.hidden)(lambda: step(turn, True))
-        pl.when(jnp.logical_not(turn.hidden))(lambda: step(turn, False))
+def run_row(ctx, core, b, step):
+    def body(n, carry):
+        turn = Turn(ctx, n // 4, (core, b, n % 4))
+        pl.when(turn.needed & turn.hidden)(lambda: step(turn, True))
+        pl.when(turn.needed & jnp.logical_not(turn.hidden))(lambda: step(turn, False))
         return carry
 
-    lax.fori_loop(start, stop, body, 0)
+    lax.fori_loop(0, 8, body, 0)
 
 
 def attend_step(turn, hidden, kv_ref, q_ref, doc_ref, m_ref, l_ref, acc_ref):
-    core, b, a = slot_of(turn.block)
+    core, b, a = turn.slot
     segment = turn.segment
     kv = kv_ref[core, b, a, 0]
     scores = turn.scores(mm(kv[:, :HD], q_ref[segment]), doc_ref, hidden)
@@ -353,7 +379,7 @@
 
 
 def attend_back_step(turn, hidden, kv_ref, q_ref, doc_ref, do_ref, lse_ref, delta_ref, dq_ref, dkv_ref):
-    core, b, a = slot_of(turn.block)
+    core, b, a = turn.slot
     segment = turn.segment
     kv = kv_ref[core, b, a, 0]
     keys, values = kv[:, :HD], kv[:, HD:]
@@ -366,7 +392,8 @@
 
 
 D, DPAD, FF_HERE, GROUP, GROUP_Q = 896, 1024, 2432, 576, 448
-QKV_W, ATTN_W, FFN_W = 640, 1152, 3 * 2432
+QKV_W, OUT_W, FFN_W = 640, 512, 3 * 2432
+ATTN_W = QKV_W + OUT_W
 GAIN_ONE, GAIN_TWO = 576, 577
 EPS_VALUE = 1e-06
 THETA = 1000000.0
@@ -424,6 +451,8 @@
 
 
 def flat(ref, start, width):
+    if not isinstance(start, int):
+        start = pl.multiple_of(start, 128)
     return ref[:, :, :, :, :, pl.ds(start, width)].reshape(DPAD, width)
 
 
@@ -437,6 +466,7 @@
 
 def forward_kernel(
     attn_row,
+    out_row,
     ffn_row,
     x_in,
     ct_in,
@@ -446,6 +476,7 @@
     doc,
     attn_full,
     ffn_full,
+    w_out,
     x_out,
     ct_out,
     ct_tokens,
@@ -456,12 +487,12 @@
     lse,
     att,
     middle,
+    outs_mine,
+    outs_full,
     q_send,
     kv_mine,
     att_send,
     att_far,
-    branch_send,
-    branch_far,
     m_ref,
     l_ref,
     acc_ref,
@@ -473,79 +504,110 @@
     attn = Gather(p, attn_row, attn_full, *sems[0:3])
     ffn = Gather(p, ffn_row, ffn_full, *sems[3:6])
     keys = Gather(p, kv_mine, kv_full, *sems[6:9])
-    greet(attn.peers() + [p.mirror, p.other_tp])
+    outs = Gather(p, outs_mine, outs_full, *sems[9:12])
+    greet(attn.peers() + [p.mirror, p.other_tp, p.mirror_tp])
     attn.begin()
+    own_out = pl.ds(pl.multiple_of(p.tp * OUT_W, 128), OUT_W)
+    out_copy = remote(out_row, outs_mine.at[:, own_out], pair_send, pair_recv, 0, p.other_tp)
+    out_copy.start()
     ffn.begin()
+    outs_mine[:, own_out] = out_row[...]
     x = mm_nt(select[...], x_in[...])
     x_out[...] = x
     attn.first()
     ct_out[...] = mm_nt(select[...], ct_in[...]).astype(BF16)
     attn.second()
-    ffn.first()
     ct_tokens[...] = mm_nt(ct_in[...], select[...]).astype(BF16)
     attn.third()
+    ffn.first()
+    m_ref[...] = jnp.full(m_ref.shape, NEGATIVE, F32)
+    l_ref[...] = jnp.zeros(l_ref.shape, F32)
+    acc_ref[...] = jnp.zeros(acc_ref.shape, F32)
     attn.fourth()
+    attn.fifth()
     ffn.second()
-    attn.fifth()
+    out_copy.wait()
     attn.finish()
-    ffn.third()
+    outs.begin()
 
     gain = flat(attn_full, 512, 128)[:, GAIN_ONE - 512 : GAIN_ONE - 511].astype(F32)
     row = lax.broadcasted_iota(jnp.int32, (DPAD, 256), 0)
     x = x_out[...]
     normed = jnp.where(row % 16 == 14, 1.0, x * inv_rms(x) * gain)
     normed_out[...] = normed.astype(BF16)
+    outs.first()
     mixed = mm(normed.T.astype(BF16), flat(attn_full, 0, QKV_W)).T
+    outs.second()
+    key = rotate(mixed[GROUP_Q : GROUP_Q + HD], cosine[...], sine[...])
+    kv_mine[...] = jnp.concatenate([key, mixed[GROUP_Q + HD : GROUP]], 0).T.astype(BF16)
+    keys.begin()
+    keys.first()
     for h in range(7):
         query = rotate(mixed[64 * h : 64 * h + 64], cosine[...], sine[...]).astype(BF16).astype(F32) * 0.125
         q_both[0, :, lanes(h)] = query[:, :128].astype(BF16)
         q_send[:, lanes(h)] = query[:, 128:].astype(BF16)
-    q_copy = remote(q_send, q_both.at[1], pair_send, pair_recv, 0, p.mirror)
+    q_copy = remote(q_send, q_both.at[1], pair_send, pair_recv, 1, p.mirror)
     q_copy.start()
-    key = rotate(mixed[GROUP_Q : GROUP_Q + HD], cosine[...], sine[...])
-    kv_mine[...] = jnp.concatenate([key, mixed[GROUP_Q + HD : GROUP]], 0).T.astype(BF16)
-    for stage in ("begin", "first", "second", "third", "fourth", "fifth", "finish"):
-        getattr(keys, stage)()
-    m_ref[...] = jnp.full(m_ref.shape, NEGATIVE, F32)
-    l_ref[...] = jnp.zeros(l_ref.shape, F32)
-    acc_ref[...] = jnp.zeros(acc_ref.shape, F32)
+    keys.second()
+    ffn.third_near()
+    outs.third()
+    keys.third()
     q_copy.wait()
-    ffn.fourth()
 
     def step(turn, hidden):
         attend_step(turn, hidden, kv_full, q_both, doc, m_ref, l_ref, acc_ref)
 
-    run_turns(p.ctx, 1, 0, 16, step)
+    run_row(p.ctx, p.core, p.b, step)
+    outs.fourth()
+    keys.fourth()
+    run_row(p.ctx, p.core, (p.b + 3) % 4, step)
+    outs.fifth()
+    keys.fifth()
+    ffn.third_rest()
+    run_row(p.ctx, p.core, (p.b + 1) % 4, step)
+    run_row(p.ctx, p.core, (p.b + 2) % 4, step)
+    ffn.fourth_near()
+    for ahead in (0, 3, 1, 2):
+        keys.from_core(ahead)
+        run_row(p.ctx, 1 - p.core, (p.a + ahead) % 4, step)
+    keys.sent()
+    attended[...] = acc_ref[...] / l_ref[...]
+    att_send[...] = attended[...].astype(BF16)
+    att_copies = [
+        remote(att_send.at[1], att_far.at[0], pair_send, pair_recv, 2, p.mirror),
+        remote(att_send.at[0], att_far.at[1], pair_send, pair_recv, 3, p.other_tp),
+        remote(att_send.at[1], att_far.at[2], pair_send, pair_recv, 4, p.mirror_tp),
+    ]
+    for copy in att_copies:
+        copy.start()
+    lse[...] = m_ref[...] + jnp.log(l_ref[...])
+    outs.finish()
+    ffn.fourth_rest()
+    w_out[...] = flat(outs_full, p.tp * OUT_W, OUT_W)
+    att[:, pl.ds(GROUP_Q, 64), :] = jnp.zeros((2, 64, 256), BF16)
+    for h in range(7):
+        att[p.tp, head(h), lanes(0)] = att_send[0, :, lanes(h)]
+    for copy in att_copies:
+        copy.wait()
+    for h in range(7):
+        att[p.tp, head(h), lanes(1)] = att_far[0, :, lanes(h)]
+        att[1 - p.tp, head(h), lanes(0)] = att_far[1, :, lanes(h)]
+        att[1 - p.tp, head(h), lanes(1)] = att_far[2, :, lanes(h)]
+    middle[...] = x_out[...] + mm(flat(outs_full, 0, 2 * OUT_W), att[...].reshape(2 * OUT_W, 256))
     ffn.fifth()
-    run_turns(p.ctx, 1, 16, TURNS, step)
-    attended[...] = acc_ref[...] / l_ref[...]
-    att_send[...] = attended[1].astype(BF16)
-    att_copy = remote(att_send, att_far, pair_send, pair_recv, 1, p.mirror)
-    att_copy.start()
-    lse[...] = m_ref[...] + jnp.log(l_ref[...])
-    att[pl.ds(GROUP_Q, 64), :] = jnp.zeros((64, 256), BF16)
-    for h in range(7):
-        att[head(h), lanes(0)] = attended[0, :, lanes(h)].astype(BF16)
-    att_copy.wait()
-    for h in range(7):
-        att[head(h), lanes(1)] = att_far[:, lanes(h)]
-    branch_send[...] = mm(flat(attn_full, QKV_W, 512), att[...]).astype(BF16)
-    branch_copy = remote(branch_send, branch_far, pair_send, pair_recv, 2, p.other_tp)
-    branch_copy.start()
     ffn.finish()
-    branch_copy.wait()
-    middle[...] = x_out[...] + (branch_send[...].astype(F32) + branch_far[...].astype(F32))
-
-
-def forward(attn_row, ffn_row, x, ct, select, cosine, sine, doc):
+
+
+def forward(*arrays):
     dma = pltpu.SemaphoreType.DMA
     gather_sems = [dma((GATHER_SEMS,)), dma((GATHER_SEMS,)), dma]
     in_vmem, in_hbm = pl.BlockSpec(memory_space=VMEM), pl.BlockSpec(memory_space=ANY)
     return pl.pallas_call(
         forward_kernel,
         out_shape=[
-            shape((2, 4, 4, 2, 16, ATTN_W), BF16),
+            shape((2, 4, 4, 2, 16, QKV_W), BF16),
             shape((2, 4, 4, 2, 16, FFN_W), BF16),
+            shape((DPAD, OUT_W), BF16),
             shape((DPAD, 256), F32),
             shape((DPAD, 256), BF16),
             shape((256, DPAD), BF16),
@@ -554,30 +616,34 @@
             shape((2, 4, 4, 1, 256, 128), BF16),
             shape((2, HD, ROWS), F32),
             shape((2, 1, ROWS), F32),
-            shape((512, 256), BF16),
+            shape((2, OUT_W, 256), BF16),
             shape((DPAD, 256), F32),
         ],
-        in_specs=[in_vmem, in_hbm] + [in_vmem] * 6,
-        out_specs=[in_vmem, in_hbm] + [in_vmem] * 10,
+        in_specs=[in_vmem, in_vmem, in_hbm] + [in_vmem] * 6,
+        out_specs=[in_vmem, in_hbm] + [in_vmem] * 11,
         scratch_shapes=[
+            VMEM((16, 2 * OUT_W), BF16),
+            VMEM((2, 4, 4, 2, 16, 2 * OUT_W), BF16),
             VMEM((HD, ROWS), BF16),
             VMEM((256, 128), BF16),
-            VMEM((HD, ROWS), BF16),
-            VMEM((HD, ROWS), BF16),
-            VMEM((DPAD, 256), BF16),
-            VMEM((DPAD, 256), BF16),
+            VMEM((2, HD, ROWS), BF16),
+            VMEM((3, HD, ROWS), BF16),
             VMEM((2, 1, ROWS), F32),
             VMEM((2, 1, ROWS), F32),
             VMEM((2, HD, ROWS), F32),
-            dma((3,)),
-            dma((3,)),
+            dma((5,)),
+            dma((5,)),
         ]
-        + gather_sems * 3,
+        + gather_sems * 4,
         compiler_params=pltpu.CompilerParams(collective_id=0, has_side_effects=True, vmem_limit_bytes=VMEM_BYTES),
-    )(attn_row, ffn_row, x, ct, select, cosine, sine, doc)
-
-
-def ffn_chunk(weights, slot, width, normed, tokens, ct, ct_tokens, part, start, out_sum, grad_sum):
+    )(*arrays)
+
+
+def tile_of(index):
+    return index // 16, (index // 4) % 4, index % 4, 0
+
+
+def ffn_chunk(weights, slot, width, tile, tokens, ct_tokens, gate_kept, up_kept, hidden_kept, out_sum, grad_sum):
     w_gate, w_up, w_down = (weights[slot, k, :, pl.ds(0, width)] for k in range(3))
     gate, up = mm(tokens[...], w_gate), mm(tokens[...], w_up)
     grad_hidden = mm(ct_tokens[...], w_down)
@@ -588,13 +654,32 @@
     grad_gate = (grad_hidden * up * sigmoid * (1.0 + gate * (1.0 - sigmoid))).astype(BF16)
     grad_sum[...] += mm_nt(w_gate, grad_gate) + mm_nt(w_up, grad_up)
     out_sum[...] += mm_nt(w_down, hidden)
-    for k, (left, right) in enumerate(((normed, grad_gate), (normed, grad_up), (ct, hidden))):
-        part[:, :, :, :, :, pl.ds(k * FF_HERE + start, width)] = unflat(mm(left[...], right).astype(BF16))
+    for k in range(width // 128):
+        part = slice(128 * k, 128 * k + 128)
+        gate_kept[tile_of(tile + k)] = grad_gate[:, part]
+        up_kept[tile_of(tile + k)] = grad_up[:, part].astype(F32)
+        hidden_kept[tile + k] = hidden[:, part]
+
+
+def ffn_weight_grads(tile, tiles, normed, ct, gate_kept, up_kept, hidden_kept, part):
+    places = [tile_of(tile + k) for k in range(tiles)]
+    pairs = (
+        (normed, [gate_kept[place] for place in places]),
+        (normed, [up_kept[place].astype(BF16) for place in places]),
+        (ct, [hidden_kept[tile + k] for k in range(tiles)]),
+    )
+    for k, (left, right) in enumerate(pairs):
+        start = k * FF_HERE + tile * 128
+        if not isinstance(start, int):
+            start = pl.multiple_of(start, 128)
+        product = mm(left[...], jnp.concatenate(right, 1) if tiles > 1 else right[0])
+        part[:, :, :, :, :, pl.ds(start, tiles * 128)] = unflat(product.astype(BF16))
 
 
 def backward_kernel(
     attn_full,
     ffn_full,
+    w_out,
     x_kept,
     ct,
     ct_tokens,
@@ -613,6 +698,7 @@
     attn_mine,
     ffn_mine,
     weights,
+    hidden_kept,
     normed_ffn,
     tokens,
     out_sum,
@@ -659,6 +745,7 @@
     for copy in load(0, 0, CHUNK):
         copy.start()
     greet(ffn.peers() + [p.mirror, p.other_tp])
+    ffn_kept = (kv_part, dkv, hidden_kept)
     gain_two = flat(attn_full, 512, 128)[:, GAIN_TWO - 512 : GAIN_TWO - 511].astype(F32)
     mid = middle[...]
     inverse = inv_rms(mid)
@@ -667,7 +754,7 @@
     tokens[...] = scaled.T.astype(BF16)
     out_sum[...] = jnp.zeros(out_sum.shape, F32)
     grad_sum[...] = jnp.zeros(grad_sum.shape, F32)
-    chunks, tail = FF_HERE // CHUNK, FF_HERE % CHUNK
+    chunks, tail, tiles = FF_HERE // CHUNK, FF_HERE % CHUNK, CHUNK // 128
 
     def chunk_body(index, carry):
         slot = index % 2
@@ -684,23 +771,25 @@
             for copy in load(chunks, chunks % 2, tail):
                 copy.start()
 
-        start = pl.multiple_of(index * CHUNK, 128)
-        ffn_chunk(weights, slot, CHUNK, normed_ffn, tokens, ct, ct_tokens, ffn_part, start, out_sum, grad_sum)
+        ffn_chunk(weights, slot, CHUNK, index * tiles, tokens, ct_tokens, *ffn_kept, out_sum, grad_sum)
         return carry
 
     lax.fori_loop(0, chunks, chunk_body, 0)
     for copy in load(chunks, chunks % 2, tail):
         copy.wait()
-    ffn_chunk(
-        weights, chunks % 2, tail, normed_ffn, tokens, ct, ct_tokens, ffn_part, chunks * CHUNK, out_sum, grad_sum
-    )
+    ffn_chunk(weights, chunks % 2, tail, chunks * tiles, tokens, ct_tokens, *ffn_kept, out_sum, grad_sum)
     grad_send[...] = grad_sum[...].astype(BF16)
     grad_copy = remote(grad_send, grad_far, pair_send, pair_recv, 0, p.other_tp)
     grad_copy.start()
+
+    def grads_body(index, carry):
+        ffn_weight_grads(index * tiles, tiles, normed_ffn, ct, *ffn_kept, ffn_part)
+        return carry
+
+    lax.fori_loop(0, chunks, grads_body, 0)
+    ffn_weight_grads(chunks * tiles, tail // 128, normed_ffn, ct, *ffn_kept, ffn_part)
     ffn.begin()
     out_send[...] = out_sum[...].astype(BF16)
-    out_copy = remote(out_send, out_far, pair_send, pair_recv, 1, p.other_tp)
-    out_copy.start()
     x, normed, grad_middle = out_sum, normed_ffn, grad_sum
     kept = [
         pltpu.make_async_copy(x_kept, x, kept_sems.at[0]),
@@ -711,6 +800,8 @@
     dq[...] = jnp.zeros(dq.shape, F32)
     dkv[...] = jnp.zeros(dkv.shape, F32)
     grad_copy.wait()
+    out_copy = remote(out_send, out_far, pair_send, pair_recv, 1, p.other_tp)
+    out_copy.start()
     mid = middle[...]
     inverse = inv_rms(mid)
     grad_normed = grad_send[...].astype(F32) + grad_far[...].astype(F32)
@@ -718,8 +809,7 @@
     gain_two_grad = jnp.sum(grad_normed * mid * inverse, 1, keepdims=True)
     grad_mid = ct[...].astype(F32) + norm_back(mid, inverse, grad_normed * gain_two)
     grad_middle[...] = grad_mid
-    w_out = flat(attn_full, QKV_W, 512)
-    grad_att = mm(grad_mid.T.astype(BF16), w_out).T
+    grad_att = mm(grad_mid.T.astype(BF16), w_out[...]).T
     for h in range(7):
         do_both[0, :, lanes(h)] = grad_att[64 * h : 64 * h + 64, :128].astype(BF16)
         do_send[:, lanes(h)] = grad_att[64 * h : 64 * h + 64, 128:].astype(BF16)
@@ -732,21 +822,38 @@
     def step(turn, hidden):
         attend_back_step(turn, hidden, kv_full, q_both, doc, do_both, lse, delta, dq, dkv)
 
-    run_turns(p.ctx, 0, 0, 10, step)
+    def far_row(ahead):
+        slot = (p.a + ahead) % 4
+        run_row(p.ctx, 1 - p.core, slot, step)
+        kv_part[1 - p.core, slot] = dkv[1 - p.core, slot].astype(BF16)
+        keys.to_core(ahead)
+
+    def own_row(ahead):
+        slot = (p.b + ahead) % 4
+        run_row(p.ctx, p.core, slot, step)
+        kv_part[p.core, slot] = dkv[p.core, slot].astype(BF16)
+
+    far_row(2)
+    far_row(1)
     ffn.second()
-    run_turns(p.ctx, 0, 10, TURNS, step)
+    far_row(3)
+    far_row(0)
+    own_row(2)
+    keys.first()
+    own_row(1)
+    own_row(3)
+    keys.second()
+    own_row(0)
+    ffn.third()
     dq_send[...] = dq[1].astype(BF16)
     dq_copy = remote(dq_send, dq_far, pair_send, pair_recv, 3, p.mirror)
     dq_copy.start()
-    kv_part[...] = dkv[...].astype(BF16)
-    keys.begin()
-    ffn.third()
-    keys.first()
     out_copy.wait()
     output[...] = (middle[...] + (out_send[...].astype(F32) + out_far[...].astype(F32))).astype(BF16)
-    keys.second()
-    attn_part[:, :, :, :, :, pl.ds(QKV_W, 512)] = unflat(mm_nt(grad_middle[...].astype(BF16), att[...]).astype(BF16))
     keys.third()
+    attn_part[:, :, :, :, :, pl.ds(QKV_W, OUT_W)] = unflat(
+        mm_nt(grad_middle[...].astype(BF16), att[p.tp]).astype(BF16)
+    )
     ffn.fourth()
     keys.fourth()
     keys.fifth()
@@ -804,10 +911,11 @@
     return pl.pallas_call(
         backward_kernel,
         out_shape=[shape(wide, BF16), shape(wide, BF16), shape((16, ATTN_W), F32), shape((16, FFN_W), F32)],
-        in_specs=[in_vmem, in_hbm, in_hbm, in_vmem, in_vmem, in_hbm] + [in_vmem] * 9,
+        in_specs=[in_vmem, in_hbm, in_vmem, in_hbm, in_vmem, in_vmem, in_hbm] + [in_vmem] * 9,
         out_specs=[in_vmem] * 4,
         scratch_shapes=[
             VMEM((2, 3, DPAD, CHUNK), BF16),
+            VMEM((FF_HERE // 128, 256, 128), BF16),
             VMEM(wide, BF16),
             VMEM(tall, BF16),
             VMEM(wide, F32),
@@ -859,16 +967,16 @@
         [
             jnp.concatenate([query_key_value_weight[:, 0], bias_row, jnp.zeros((1, GROUP), BF16)], 0),
             jnp.pad(jnp.stack([gain_attn, gain_ffn], 1), ((0, 2), (0, 62))),
-            jnp.pad(output_weight[0].T, ((0, 2), (0, 64))),
         ],
         1,
     )
+    out_row = jnp.pad(output_weight[0].T, ((0, 2), (0, 64)))
     ffn_row = jnp.pad(jnp.concatenate([gate_weight, up_weight, down_weight.T], 1), ((0, 2), (0, 0)))
     cosine, sine = rope_tables(positions[0])
     row = lax.axis_index("ctx") * 256 + jnp.arange(128, dtype=jnp.int32)
     doc = jnp.stack([jnp.tile((row - positions[0, :128])[None], (1, 7)), jnp.full((1, ROWS), 128, jnp.int32)])
     attn_full, ffn_full, *kept = forward(
-        attn_row, ffn_row, inputs[0], cotangent[0], select, cosine, sine, doc
+        attn_row, out_row, ffn_row, inputs[0], cotangent[0], select, cosine, sine, doc
     )
     output, grad_inputs, attn, ffn = backward(
         attn_full, ffn_full.reshape(DPAD, FFN_W), *kept, cosine, sine, doc

time: 273 us -> 264 us (0.967)
  Pallas kernels: 253 us -> 241 us
    pallas_call x1, Pallas kernels: 116 us -> 97.9 us  [forward(): pl.pallas_call(forward_kernel, out_shape=[shape((2, 4, 4, 2, 16, QKV_W),...]
    pallas_call x1, Pallas kernels: 137 us -> 144 us  [backward(): pl.pallas_call(backward_kernel, out_shape=[shape(wide, BF16), shape(wide,...]
where the time goes in v3:
time: 264 us; the launch traced here: 260 us
  Pallas kernels  241 us (91%)
  local copies, waits for them, and re-layouts  8 us (3%)
  other arithmetic  6.02 us (2%)
  matrix products  4.04 us (2%)
    pallas_call x1, Pallas kernels, backward(): pl.pallas_call(backward_kernel, out_shape=[shape(wide, BF16), shape(wide,...  144 us
    pallas_call x1, Pallas kernels, forward(): pl.pallas_call(forward_kernel, out_shape=[shape((2, 4, 4, 2, 16, QKV_W),...  97.9 us

profile of v3, /device:TPU:8, one launch (start us, length us, event | category | flops | bytes accessed | tf_op | source)
XLA Modules:
  0.0 260.5 jit_solution(4943917507311690783)
XLA Ops:
  0.7 0.9 dynamic_update_slice.3
  1.5 0.7 pad_maximum_fusion.1
  2.2 0.1 copy.31
  2.3 1.4 fusion.10.attn_row
  3.8 0.7 bitcast_subtract_fusion
  4.4 0.6 stack.15.doc
  5.0 0.7 convert_element_type.16
  5.7 0.1 broadcast_multiply_fusion
  5.8 0.8 fusion.7
  6.6 1.7 fusion.6.ffn_row
  8.3 1.3 pad.14.out_row
  9.6 97.9 %shard_map.203 = (bf16[2,4,4,2,16,640]{5,4,3,2,1,0:T(8,128)(2,1)}, bf16[2,4,4,2,16,7296]{5,4,3,2,1,0:T(8,128)(2,1)}, bf16[1024,512]{1,0:T(8,128)(2,1)}, f32[1024...) custom-call(bf16[16,640]{1,0:T(8,128)(2,1)} %fusion.10.attn_row, ...), custom_call_target="tpu_custom_call" | custom-call | tf_op jit(solution)/shard_map/pallas_call | solution.py:605
  107.5 0.0 copy-start
  107.5 143.6 %shard_map.204 = (bf16[1024,256]{1,0:T(8,128)(2,1)}, bf16[1024,256]{1,0:T(8,128)(2,1)}, f32[16,1152]{1,0:T(8,128)}, f32[16,7296]{1,0:T(8,128)}) custom-call(bf16[2,4,4,2,16,640]{5,4,3,2,1,0:T(8,128)(2,1)} %get-tuple-element.28.attn_full, bf16[1024,7296]{1,0:T(8,128)(2,1)} %bitcast.29, bf16[1024,512]{1,0:T(8,128)(2,1)} %get-tuple-element.30.w_out, ...), custom_call_target="tpu_custom_call" | custom-call | tf_op jit(solution)/shard_map/pallas_call | solution.py:911
  251.1 0.0 copy-start.1
  251.1 1.9 slice_bitcast_fusion
  253.0 0.0 copy-done
  253.0 2.5 fusion
  255.6 0.0 copy-start.2
  255.6 0.0 copy-done.1
  255.6 1.5 fusion.1
  257.1 0.0 copy-done.2
  257.1 0.7 copy.32
  257.8 0.6 copy.33
  258.4 0.6 constant_dynamic-slice_fusion.1
  259.0 0.6 constant_dynamic-slice_fusion
  259.6 0.7 slice_reduce_fusion
  (7 shorter events, 0.0 us)
Async XLA Ops:
  107.5 145.5 %copy-start = (bf16[1024,896]{1,0:T(8,128)(2,1)S(1)}, bf16[1024,896]{1,0:T(8,128)(2,1)}, u32[]{:S(2)}) copy-start(bf16[1024,896]{1,0:T(8,128)(2,1)} %constant.41.clone.select) | copy-start | bytes 5505028
  251.1 4.5 %copy-start.1 = (bf16[1024,256]{1,0:T(8,128)(2,1)S(1)}, bf16[1024,256]{1,0:T(8,128)(2,1)}, u32[]{:S(2)}) copy-start(bf16[1024,256]{1,0:T(8,128)(2,1)} %get-tuple-element.42) | copy-start | bytes 1572868
  255.6 1.5 copy-start.2

commit v4 on v3

--- a/solution.py
+++ b/solution.py
@@ -345,12 +345,12 @@
         self.needed = self.block < count
         self.hidden = (self.block == 0) | (self.block == count - 1)
 
-    def scores(self, scores, doc_ref, hidden):
+    def scores(self, scores, doc_ref, hidden, part=slice(0, ROWS)):
         if not hidden:
             return scores
-        key = lax.broadcasted_iota(jnp.int32, (256, ROWS), 0) + self.block * 256
-        row = lax.broadcasted_iota(jnp.int32, (256, ROWS), 1) % 128 + self.first_row
-        visible = (key <= row) & (key >= doc_ref[self.segment])
+        key = lax.broadcasted_iota(jnp.int32, scores.shape, 0) + self.block * 256
+        row = (lax.broadcasted_iota(jnp.int32, scores.shape, 1) + part.start) % 128 + self.first_row
+        visible = (key <= row) & (key >= doc_ref[self.segment, :, part])
         return jnp.where(visible, scores, NEGATIVE)
 
 
@@ -368,14 +368,22 @@
     core, b, a = turn.slot
     segment = turn.segment
     kv = kv_ref[core, b, a, 0]
-    scores = turn.scores(mm(kv[:, :HD], q_ref[segment]), doc_ref, hidden)
-    old = m_ref[segment]
-    new = jnp.maximum(old, jnp.max(scores, 0, keepdims=True))
-    probs = jnp.exp(scores - new)
-    keep = jnp.exp(old - new)
-    m_ref[segment] = new
-    l_ref[segment] = l_ref[segment] * keep + jnp.sum(probs, 0, keepdims=True)
-    acc_ref[segment] = acc_ref[segment] * keep + mm(kv[:, HD:].T, probs.astype(BF16))
+    keys, values_t = kv[:, :HD], kv[:, HD:].T
+    q, old_max, old_sum, old_acc = q_ref[segment], m_ref[segment], l_ref[segment], acc_ref[segment]
+    parts = [slice(start, min(start + 256, ROWS)) for start in range(0, ROWS, 256)]
+    products = [turn.scores(mm(keys, q[:, part]), doc_ref, hidden, part) for part in parts]
+    results = []
+    for part, scores in zip(parts, products):
+        old = old_max[:, part]
+        new = jnp.maximum(old, jnp.max(scores, 0, keepdims=True))
+        probs = jnp.exp(scores - new)
+        keep = jnp.exp(old - new)
+        total = old_sum[:, part] * keep + jnp.sum(probs, 0, keepdims=True)
+        results.append((new, total, old_acc[:, part] * keep + mm(values_t, probs.astype(BF16))))
+    for part, (new, total, acc) in zip(parts, results):
+        m_ref[segment, :, part] = new
+        l_ref[segment, :, part] = total
+        acc_ref[segment, :, part] = acc
 
 
 def attend_back_step(turn, hidden, kv_ref, q_ref, doc_ref, do_ref, lse_ref, delta_ref, dq_ref, dkv_ref):
@@ -399,6 +407,7 @@
 THETA = 1000000.0
 VMEM_BYTES = 62 << 20
 CHUNK = 256
+DEPTH = 3
 
 
 def slot_columns():
@@ -409,10 +418,6 @@
     columns = np.full((64, 16), -1)
     columns[slot, :14] = index[:, None] * 14 + np.arange(14)
     return columns.reshape(-1)
-
-
-def mm_tn(left, right):
-    return lax.dot_general(left, right, (((0,), (0,)), ((), ())), preferred_element_type=F32)
 
 
 def rope_tables(positions):
@@ -474,19 +479,27 @@
     cosine,
     sine,
     doc,
-    attn_full,
+    attn_out,
     ffn_full,
     w_out,
+    x_kept,
+    ct_kept,
+    tokens_kept,
+    normed_kept,
+    q_kept,
+    kv_kept,
+    attended,
+    lse,
+    att,
+    middle,
+    attn_full,
     x_out,
     ct_out,
     ct_tokens,
     normed_out,
     q_both,
     kv_full,
-    attended,
-    lse,
-    att,
-    middle,
+    keep_sems,
     outs_mine,
     outs_full,
     q_send,
@@ -501,6 +514,13 @@
     *sems,
 ):
     p = Place()
+    kept = []
+
+    def keep(ref, out):
+        copy = pltpu.make_async_copy(ref, out, keep_sems.at[len(kept)])
+        copy.start()
+        kept.append(copy)
+
     attn = Gather(p, attn_row, attn_full, *sems[0:3])
     ffn = Gather(p, ffn_row, ffn_full, *sems[3:6])
     keys = Gather(p, kv_mine, kv_full, *sems[6:9])
@@ -514,10 +534,13 @@
     outs_mine[:, own_out] = out_row[...]
     x = mm_nt(select[...], x_in[...])
     x_out[...] = x
+    keep(x_out, x_kept)
     attn.first()
     ct_out[...] = mm_nt(select[...], ct_in[...]).astype(BF16)
+    keep(ct_out, ct_kept)
     attn.second()
     ct_tokens[...] = mm_nt(ct_in[...], select[...]).astype(BF16)
+    keep(ct_tokens, tokens_kept)
     attn.third()
     ffn.first()
     m_ref[...] = jnp.full(m_ref.shape, NEGATIVE, F32)
@@ -529,12 +552,14 @@
     out_copy.wait()
     attn.finish()
     outs.begin()
+    keep(attn_full, attn_out)
 
     gain = flat(attn_full, 512, 128)[:, GAIN_ONE - 512 : GAIN_ONE - 511].astype(F32)
     row = lax.broadcasted_iota(jnp.int32, (DPAD, 256), 0)
     x = x_out[...]
     normed = jnp.where(row % 16 == 14, 1.0, x * inv_rms(x) * gain)
     normed_out[...] = normed.astype(BF16)
+    keep(normed_out, normed_kept)
     outs.first()
     mixed = mm(normed.T.astype(BF16), flat(attn_full, 0, QKV_W)).T
     outs.second()
@@ -549,10 +574,10 @@
     q_copy = remote(q_send, q_both.at[1], pair_send, pair_recv, 1, p.mirror)
     q_copy.start()
     keys.second()
-    ffn.third_near()
     outs.third()
     keys.third()
     q_copy.wait()
+    keep(q_both, q_kept)
 
     def step(turn, hidden):
         attend_step(turn, hidden, kv_full, q_both, doc, m_ref, l_ref, acc_ref)
@@ -563,14 +588,17 @@
     run_row(p.ctx, p.core, (p.b + 3) % 4, step)
     outs.fifth()
     keys.fifth()
+    ffn.third_near()
     ffn.third_rest()
     run_row(p.ctx, p.core, (p.b + 1) % 4, step)
     run_row(p.ctx, p.core, (p.b + 2) % 4, step)
-    ffn.fourth_near()
     for ahead in (0, 3, 1, 2):
         keys.from_core(ahead)
+        if ahead == 1:
+            ffn.fourth_near()
         run_row(p.ctx, 1 - p.core, (p.a + ahead) % 4, step)
     keys.sent()
+    keep(kv_full, kv_kept)
     attended[...] = acc_ref[...] / l_ref[...]
     att_send[...] = attended[...].astype(BF16)
     att_copies = [
@@ -596,6 +624,8 @@
     middle[...] = x_out[...] + mm(flat(outs_full, 0, 2 * OUT_W), att[...].reshape(2 * OUT_W, 256))
     ffn.fifth()
     ffn.finish()
+    for copy in kept:
+        copy.wait()
 
 
 def forward(*arrays):
@@ -620,8 +650,16 @@
             shape((DPAD, 256), F32),
         ],
         in_specs=[in_vmem, in_vmem, in_hbm] + [in_vmem] * 6,
-        out_specs=[in_vmem, in_hbm] + [in_vmem] * 11,
+        out_specs=[in_hbm, in_hbm, in_vmem] + [in_hbm] * 6 + [in_vmem] * 4,
         scratch_shapes=[
+            VMEM((2, 4, 4, 2, 16, QKV_W), BF16),
+            VMEM((DPAD, 256), F32),
+            VMEM((DPAD, 256), BF16),
+            VMEM((256, DPAD), BF16),
+            VMEM((DPAD, 256), BF16),
+            VMEM((2, HD, ROWS), BF16),
+            VMEM((2, 4, 4, 1, 256, 128), BF16),
+            dma((7,)),
             VMEM((16, 2 * OUT_W), BF16),
             VMEM((2, 4, 4, 2, 16, 2 * OUT_W), BF16),
             VMEM((HD, ROWS), BF16),
@@ -677,26 +715,35 @@
 
 
 def backward_kernel(
-    attn_full,
+    attn_kept,
     ffn_full,
-    w_out,
+    w_out_kept,
     x_kept,
-    ct,
+    ct_kept,
     ct_tokens,
     normed_kept,
-    q_both,
-    kv_full,
-    attended,
+    q_kept,
+    kv_kept,
+    attended_kept,
     lse,
-    att,
+    att_kept,
     middle,
     cosine,
     sine,
     doc,
+    select,
     output,
     grad_inputs,
     attn_mine,
     ffn_mine,
+    attn_full,
+    w_out,
+    ct,
+    q_both,
+    kv_full,
+    attended,
+    att,
+    late_sems,
     weights,
     hidden_kept,
     normed_ffn,
@@ -725,7 +772,7 @@
     *scratch,
 ):
     p = Place()
-    out_send, grad_send, do_send = output, grad_inputs, dq_send
+    out_send, grad_send, do_send = weights.at[2, 0], weights.at[2, 1], dq_send
     ffn = Scatter(p, ffn_part, scratch[0:6])
     keys = Scatter(p, kv_part, scratch[6:12])
     attn = Scatter(p, attn_part, scratch[12:18])
@@ -742,10 +789,25 @@
             )
         return copies
 
-    for copy in load(0, 0, CHUNK):
+    pairs = (
+        (attn_kept, attn_full),
+        (ct_kept, ct),
+        (w_out_kept, w_out),
+        (q_kept, q_both),
+        (kv_kept, kv_full),
+        (attended_kept, attended),
+        (att_kept, att),
+    )
+    late = [pltpu.make_async_copy(src, dst, late_sems.at[k]) for k, (src, dst) in enumerate(pairs)]
+    late[0].start()
+    for index in range(DEPTH - 1):
+        for copy in load(index, index, CHUNK):
+            copy.start()
+    for copy in late[1:]:
         copy.start()
     greet(ffn.peers() + [p.mirror, p.other_tp])
     ffn_kept = (kv_part, dkv, hidden_kept)
+    late[0].wait()
     gain_two = flat(attn_full, 512, 128)[:, GAIN_TWO - 512 : GAIN_TWO - 511].astype(F32)
     mid = middle[...]
     inverse = inv_rms(mid)
@@ -757,30 +819,33 @@
     chunks, tail, tiles = FF_HERE // CHUNK, FF_HERE % CHUNK, CHUNK // 128
 
     def chunk_body(index, carry):
-        slot = index % 2
+        slot, ahead = index % DEPTH, index + DEPTH - 1
         for copy in load(index, slot, CHUNK):
             copy.wait()
 
-        @pl.when(index < chunks - 1)
+        @pl.when(ahead < chunks)
         def _():
-            for copy in load(index + 1, 1 - slot, CHUNK):
+            for copy in load(ahead, ahead % DEPTH, CHUNK):
                 copy.start()
 
-        @pl.when(index == chunks - 1)
+        @pl.when(ahead == chunks)
         def _():
-            for copy in load(chunks, chunks % 2, tail):
+            for copy in load(chunks, chunks % DEPTH, tail):
                 copy.start()
 
         ffn_chunk(weights, slot, CHUNK, index * tiles, tokens, ct_tokens, *ffn_kept, out_sum, grad_sum)
         return carry
 
     lax.fori_loop(0, chunks, chunk_body, 0)
-    for copy in load(chunks, chunks % 2, tail):
+    for copy in load(chunks, chunks % DEPTH, tail):
         copy.wait()
-    ffn_chunk(weights, chunks % 2, tail, chunks * tiles, tokens, ct_tokens, *ffn_kept, out_sum, grad_sum)
+    ffn_chunk(weights, chunks % DEPTH, tail, chunks * tiles, tokens, ct_tokens, *ffn_kept, out_sum, grad_sum)
     grad_send[...] = grad_sum[...].astype(BF16)
     grad_copy = remote(grad_send, grad_far, pair_send, pair_recv, 0, p.other_tp)
     grad_copy.start()
+
+    for copy in late[1:]:
+        copy.wait()
 
     def grads_body(index, carry):
         ffn_weight_grads(index * tiles, tiles, normed_ffn, ct, *ffn_kept, ffn_part)
@@ -795,6 +860,16 @@
         pltpu.make_async_copy(x_kept, x, kept_sems.at[0]),
         pltpu.make_async_copy(normed_kept, normed, kept_sems.at[1]),
     ]
+    columns = [pl.ds(start, min(CHUNK, D - start)) for start in range(0, D, CHUNK)]
+    picks = [weights.at[k // 3, k % 3, :, pl.ds(0, column.size)] for k, column in enumerate(columns)]
+    for k, column in enumerate(columns):
+        kept.append(pltpu.make_async_copy(select.at[:, column], picks[k], kept_sems.at[2 + k]))
+
+    def put_features(out, value):
+        value = value.T.astype(BF16)
+        for column, pick in zip(columns, picks):
+            out[:, column] = mm(value, pick[...]).astype(BF16)
+
     for copy in kept:
         copy.start()
     dq[...] = jnp.zeros(dq.shape, F32)
@@ -844,21 +919,22 @@
     own_row(3)
     keys.second()
     own_row(0)
-    ffn.third()
     dq_send[...] = dq[1].astype(BF16)
     dq_copy = remote(dq_send, dq_far, pair_send, pair_recv, 3, p.mirror)
     dq_copy.start()
     out_copy.wait()
-    output[...] = (middle[...] + (out_send[...].astype(F32) + out_far[...].astype(F32))).astype(BF16)
+    for copy in kept:
+        copy.wait()
+    put_features(output, middle[...] + (out_send[...].astype(F32) + out_far[...].astype(F32)))
     keys.third()
+    ffn.third()
     attn_part[:, :, :, :, :, pl.ds(QKV_W, OUT_W)] = unflat(
         mm_nt(grad_middle[...].astype(BF16), att[p.tp]).astype(BF16)
     )
-    ffn.fourth()
     keys.fourth()
     keys.fifth()
+    ffn.fourth()
     keys.finish(kv_mine)
-    ffn.fifth()
     dq_copy.wait()
     grad_mixed[pl.ds(GROUP, QKV_W - GROUP), :] = jnp.zeros((QKV_W - GROUP, 256), BF16)
     for h in range(7):
@@ -875,8 +951,6 @@
     pl.semaphore_wait(grad_free, 1)
     grad_copy = remote(grad_send, grad_far, pair_send, pair_recv, 4, p.other_tp)
     grad_copy.start()
-    for copy in kept:
-        copy.wait()
     value = x[...]
     inverse = inv_rms(value)
     gain_one_grad = jnp.sum(grad_normed * value * inverse, 1, keepdims=True)
@@ -885,19 +959,20 @@
     grad_qkv = jnp.where(lane == GAIN_ONE, gain_one_grad, jnp.where(lane == GAIN_TWO, gain_two_grad, grad_qkv))
     attn_part[:, :, :, :, :, pl.ds(0, QKV_W)] = unflat(grad_qkv.astype(BF16))
     attn.begin()
-    ffn.finish(ffn_mine)
     attn.first()
+    ffn.fifth()
     attn.second()
     grad_copy.wait()
     gain_one = flat(attn_full, 512, 128)[:, GAIN_ONE - 512 : GAIN_ONE - 511].astype(F32)
     scaled = (grad_send[...].astype(F32) + grad_far[...].astype(F32)) * gain_one
-    grad_inputs[...] = (grad_middle[...] + norm_back(value, inverse, scaled)).astype(BF16)
+    put_features(grad_inputs, grad_middle[...] + norm_back(value, inverse, scaled))
     attn.third()
     attn.fourth()
     attn.fifth()
     attn.finish(attn_mine)
     gains_copy = remote(attn_mine.at[:, pl.ds(512, 128)], gains_far, pair_send, pair_recv, 5, p.other_tp)
     gains_copy.start()
+    ffn.finish(ffn_mine)
     gains_copy.wait()
     mine = attn_mine[:, pl.ds(512, 128)]
     lane = lax.broadcasted_iota(jnp.int32, (16, 128), 1) + 512
@@ -910,11 +985,19 @@
     wide, tall, low = (DPAD, 256), (256, DPAD), (2, HD, ROWS)
     return pl.pallas_call(
         backward_kernel,
-        out_shape=[shape(wide, BF16), shape(wide, BF16), shape((16, ATTN_W), F32), shape((16, FFN_W), F32)],
-        in_specs=[in_vmem, in_hbm, in_vmem, in_hbm, in_vmem, in_vmem, in_hbm] + [in_vmem] * 9,
+        out_shape=[shape((256, D), BF16), shape((256, D), BF16), shape((16, ATTN_W), F32), shape((16, FFN_W), F32)],
+        in_specs=[in_hbm] * 5 + [in_vmem] + [in_hbm] * 4 + [in_vmem, in_hbm] + [in_vmem] * 4 + [in_hbm],
         out_specs=[in_vmem] * 4,
         scratch_shapes=[
-            VMEM((2, 3, DPAD, CHUNK), BF16),
+            VMEM((2, 4, 4, 2, 16, QKV_W), BF16),
+            VMEM((DPAD, OUT_W), BF16),
+            VMEM(wide, BF16),
+            VMEM(low, BF16),
+            VMEM((2, 4, 4, 1, 256, 128), BF16),
+            VMEM(low, F32),
+            VMEM((2, OUT_W, 256), BF16),
+            dma((7,)),
+            VMEM((DEPTH, 3, DPAD, CHUNK), BF16),
             VMEM((FF_HERE // 128, 256, 128), BF16),
             VMEM(wide, BF16),
             VMEM(tall, BF16),
@@ -935,8 +1018,8 @@
             VMEM((2, 4, 4, 2, 16, ATTN_W), BF16),
             VMEM((16, 128), F32),
             pltpu.SemaphoreType.REGULAR,
-            dma((2, 3)),
-            dma((2,)),
+            dma((DEPTH, 3)),
+            dma((6,)),
             dma((6,)),
             dma((6,)),
         ]
@@ -961,15 +1044,13 @@
     cotangent,
 ):
     me = lax.axis_index("seq") * 32 + lax.axis_index("ctx")
-    select = jnp.asarray(slot_columns()[:, None] == np.arange(D)[None, :], BF16)
-    bias_row = lax.dynamic_update_slice(jnp.zeros((1, GROUP), BF16), query_key_value_bias, (0, 9 * me))
-    attn_row = jnp.concatenate(
-        [
-            jnp.concatenate([query_key_value_weight[:, 0], bias_row, jnp.zeros((1, GROUP), BF16)], 0),
-            jnp.pad(jnp.stack([gain_attn, gain_ffn], 1), ((0, 2), (0, 62))),
-        ],
-        1,
+    select = (slot_columns()[:, None] == np.arange(D)[None, :]).astype(BF16)
+    attn_row = (
+        jnp.pad(query_key_value_weight[:, 0], ((0, 2), (0, QKV_W - GROUP)))
+        + jnp.pad(gain_attn[:, None], ((0, 2), (GAIN_ONE, QKV_W - GAIN_ONE - 1)))
+        + jnp.pad(gain_ffn[:, None], ((0, 2), (GAIN_TWO, QKV_W - GAIN_TWO - 1)))
     )
+    attn_row = lax.dynamic_update_slice(attn_row, query_key_value_bias, (14, 9 * me))
     out_row = jnp.pad(output_weight[0].T, ((0, 2), (0, 64)))
     ffn_row = jnp.pad(jnp.concatenate([gate_weight, up_weight, down_weight.T], 1), ((0, 2), (0, 0)))
     cosine, sine = rope_tables(positions[0])
@@ -979,11 +1060,11 @@
         attn_row, out_row, ffn_row, inputs[0], cotangent[0], select, cosine, sine, doc
     )
     output, grad_inputs, attn, ffn = backward(
-        attn_full, ffn_full.reshape(DPAD, FFN_W), *kept, cosine, sine, doc
+        attn_full, ffn_full.reshape(DPAD, FFN_W), *kept, cosine, sine, doc, select
     )
     return (
-        mm_tn(output, select).astype(BF16)[None],
-        mm_tn(grad_inputs, select).astype(BF16)[None],
+        output[None],
+        grad_inputs[None],
         attn[:14, None, :GROUP],
         lax.dynamic_slice(attn, (14, 8 * me), (1, 8)),
         lax.dynamic_slice(attn, (14, 512 + me), (1, 1)),

time: 264 us -> 259 us (0.981)
  Pallas kernels: 241 us -> 233 us
  local copies, waits for them, and re-layouts: 8 us -> 15.6 us
  matrix products: 4.04 us -> 0 us
    pallas_call x1, Pallas kernels: 144 us -> 136 us  [backward(): pl.pallas_call(backward_kernel, out_shape=[shape((256, D), BF16), shape((...]
    dot_general x2 -> x0, matrix products: 4.04 us -> none  [mm_tn(): lax.dot_general(left, right, (((0,), (0,)), ((), ())), preferred_element_...]
where the time goes in v4:
time: 259 us; the launch traced here: 255 us
  Pallas kernels  233 us (90%)
  local copies, waits for them, and re-layouts  15.6 us (6%)
  other arithmetic  4.73 us (2%)
    pallas_call x1, Pallas kernels, backward(): pl.pallas_call(backward_kernel, out_shape=[shape((256, D), BF16), shape((...  136 us
    pallas_call x1, Pallas kernels, forward(): pl.pallas_call(forward_kernel, out_shape=[shape((2, 4, 4, 2, 16, QKV_W),...  97.1 us

profile of v4, /device:TPU:8, one launch (start us, length us, event | category | flops | bytes accessed | tf_op | source)
XLA Modules:
  0.0 254.6 jit_solution(15335725352357243999)
XLA Ops:
  0.7 0.7 copy.27
  1.4 0.8 copy.28
  2.2 0.8 pad_add_fusion
  3.0 0.9 dynamic_update_slice.3.attn_row
  3.8 0.0 copy-start.1
  3.9 0.7 bitcast_subtract_fusion
  4.5 0.6 stack.3.doc
  5.1 0.7 convert_element_type.14
  5.8 0.1 broadcast_multiply_fusion
  5.9 0.8 fusion.5
  6.7 1.7 fusion.4.ffn_row
  8.4 1.3 pad.24.out_row
  9.7 0.0 copy-done.1
  9.7 97.1 %shard_map.203 = (bf16[2,4,4,2,16,640]{5,4,3,2,1,0:T(8,128)(2,1)}, bf16[2,4,4,2,16,7296]{5,4,3,2,1,0:T(8,128)(2,1)}, bf16[1024,512]{1,0:T(8,128)(2,1)}, f32[1024...) custom-call(bf16[16,640]{1,0:T(8,128)(2,1)} %copy-done.1, ...), custom_call_target="tpu_custom_call" | custom-call | tf_op jit(solution)/shard_map/pallas_call | solution.py:635
  106.8 136.3 %shard_map.204 = (bf16[256,896]{1,0:T(8,128)(2,1)}, bf16[256,896]{1,0:T(8,128)(2,1)}, f32[16,1152]{1,0:T(8,128)}, f32[16,7296]{1,0:T(8,128)}) custom-call(bf16[2,4,4,2,16,640]{5,4,3,2,1,0:T(8,128)(2,1)} %get-tuple-element.28.attn_kept, bf16[1024,7296]{1,0:T(8,128)(2,1)} %bitcast.23, bf16[1024,512]{1,0:T(8,128)(2,1)} %get-tuple-element.30.w_out_kept, ...), custom_call_target="tpu_custom_call" | custom-call | tf_op jit(solution)/shard_map/pallas_call | solution.py:986
  243.1 0.0 copy-start
  243.1 1.9 slice_bitcast_fusion
  245.0 0.8 slice_bitcast_fusion.1
  245.8 0.7 copy.29
  246.5 0.8 slice_bitcast_fusion.2
  247.2 0.6 copy.30
  247.9 1.3 constant_dynamic-slice_fusion.1
  249.1 1.3 constant_dynamic-slice_fusion
  250.4 1.5 slice_reduce_fusion
  251.9 1.8 copy.34
  253.7 0.0 copy-done
  253.7 0.8 copy.35
  (3 shorter events, 0.0 us)
Async XLA Ops:
  3.8 5.9 %copy-start.1 = (bf16[16,640]{1,0:T(8,128)(2,1)}, bf16[16,640]{1,0:T(8,128)(2,1)S(1)}, u32[]{:S(2)}) copy-start(bf16[16,640]{1,0:T(8,128)(2,1)S(1)} %dynamic_update_slice.3.attn_row) | copy-start | bytes 61444
  243.1 10.6 %copy-start = (bf16[256,896]{1,0:T(8,128)(2,1)S(1)}, bf16[256,896]{1,0:T(8,128)(2,1)}, u32[]{:S(2)}) copy-start(bf16[256,896]{1,0:T(8,128)(2,1)} %get-tuple-element.42) | copy-start | bytes 1376260

commit v5 on v4

--- a/solution.py
+++ b/solution.py
@@ -469,16 +469,22 @@
     return jax.ShapeDtypeStruct(dims, dtype)
 
 
+def fill_doc(doc, positions, p):
+    row = lax.broadcasted_iota(jnp.int32, (1, 128), 1) + p.ctx * 256
+    doc[0] = jnp.concatenate([row - positions[:, :128]] * 7, 1)
+    doc[1] = jnp.full((1, ROWS), 128, jnp.int32)
+
+
 def forward_kernel(
     attn_row,
     out_row,
     ffn_row,
-    x_in,
-    ct_in,
-    select,
+    x_given,
+    ct_given,
+    select_given,
     cosine,
     sine,
-    doc,
+    positions,
     attn_out,
     ffn_full,
     w_out,
@@ -500,6 +506,11 @@
     q_both,
     kv_full,
     keep_sems,
+    doc,
+    x_in,
+    ct_in,
+    select,
+    given_sems,
     outs_mine,
     outs_full,
     q_send,
@@ -514,6 +525,10 @@
     *sems,
 ):
     p = Place()
+    pairs = ((select_given, select), (x_given, x_in), (ct_given, ct_in))
+    given = [pltpu.make_async_copy(src, dst, given_sems.at[k]) for k, (src, dst) in enumerate(pairs)]
+    for copy in given:
+        copy.start()
     kept = []
 
     def keep(ref, out):
@@ -532,6 +547,9 @@
     out_copy.start()
     ffn.begin()
     outs_mine[:, own_out] = out_row[...]
+    fill_doc(doc, positions, p)
+    for copy in given:
+        copy.wait()
     x = mm_nt(select[...], x_in[...])
     x_out[...] = x
     keep(x_out, x_kept)
@@ -649,7 +667,7 @@
             shape((2, OUT_W, 256), BF16),
             shape((DPAD, 256), F32),
         ],
-        in_specs=[in_vmem, in_vmem, in_hbm] + [in_vmem] * 6,
+        in_specs=[in_vmem, in_vmem] + [in_hbm] * 4 + [in_vmem] * 3,
         out_specs=[in_hbm, in_hbm, in_vmem] + [in_hbm] * 6 + [in_vmem] * 4,
         scratch_shapes=[
             VMEM((2, 4, 4, 2, 16, QKV_W), BF16),
@@ -660,6 +678,11 @@
             VMEM((2, HD, ROWS), BF16),
             VMEM((2, 4, 4, 1, 256, 128), BF16),
             dma((7,)),
+            VMEM((2, 1, ROWS), jnp.int32),
+            VMEM((256, D), BF16),
+            VMEM((256, D), BF16),
+            VMEM((DPAD, D), BF16),
+            dma((3,)),
             VMEM((16, 2 * OUT_W), BF16),
             VMEM((2, 4, 4, 2, 16, 2 * OUT_W), BF16),
             VMEM((HD, ROWS), BF16),
@@ -730,7 +753,7 @@
     middle,
     cosine,
     sine,
-    doc,
+    positions,
     select,
     output,
     grad_inputs,
@@ -744,6 +767,7 @@
     attended,
     att,
     late_sems,
+    doc,
     weights,
     hidden_kept,
     normed_ffn,
@@ -808,6 +832,7 @@
     greet(ffn.peers() + [p.mirror, p.other_tp])
     ffn_kept = (kv_part, dkv, hidden_kept)
     late[0].wait()
+    fill_doc(doc, positions, p)
     gain_two = flat(attn_full, 512, 128)[:, GAIN_TWO - 512 : GAIN_TWO - 511].astype(F32)
     mid = middle[...]
     inverse = inv_rms(mid)
@@ -997,6 +1022,7 @@
             VMEM(low, F32),
             VMEM((2, OUT_W, 256), BF16),
             dma((7,)),
+            VMEM((2, 1, ROWS), jnp.int32),
             VMEM((DEPTH, 3, DPAD, CHUNK), BF16),
             VMEM((FF_HERE // 128, 256, 128), BF16),
             VMEM(wide, BF16),
@@ -1054,13 +1080,11 @@
     out_row = jnp.pad(output_weight[0].T, ((0, 2), (0, 64)))
     ffn_row = jnp.pad(jnp.concatenate([gate_weight, up_weight, down_weight.T], 1), ((0, 2), (0, 0)))
     cosine, sine = rope_tables(positions[0])
-    row = lax.axis_index("ctx") * 256 + jnp.arange(128, dtype=jnp.int32)
-    doc = jnp.stack([jnp.tile((row - positions[0, :128])[None], (1, 7)), jnp.full((1, ROWS), 128, jnp.int32)])
     attn_full, ffn_full, *kept = forward(
-        attn_row, out_row, ffn_row, inputs[0], cotangent[0], select, cosine, sine, doc
+        attn_row, out_row, ffn_row, inputs[0], cotangent[0], select, cosine, sine, positions
     )
     output, grad_inputs, attn, ffn = backward(
-        attn_full, ffn_full.reshape(DPAD, FFN_W), *kept, cosine, sine, doc, select
+        attn_full, ffn_full.reshape(DPAD, FFN_W), *kept, cosine, sine, positions, select
     )
     return (
         output[None],

time: 259 us -> 257 us (level)
  no operation moved by 1% of the time
where the time goes in v5:
time: 257 us; the launch traced here: 253 us
  Pallas kernels  233 us (91%)
  local copies, waits for them, and re-layouts  15 us (6%)
  other arithmetic  4.07 us (2%)
    pallas_call x1, Pallas kernels, backward(): pl.pallas_call(backward_kernel, out_shape=[shape((256, D), BF16), shape((...  136 us
    pallas_call x1, Pallas kernels, forward(): pl.pallas_call(forward_kernel, out_shape=[shape((2, 4, 4, 2, 16, QKV_W),...  96.1 us

profile of v5, /device:TPU:8, one launch (start us, length us, event | category | flops | bytes accessed | tf_op | source)
XLA Modules:
  0.0 252.5 jit_solution(7021354278002332124)
XLA Ops:
  0.6 0.7 copy.27
  1.4 0.8 copy.28
  2.2 0.8 pad_add_fusion
  3.0 0.9 dynamic_update_slice.3.attn_row
  3.8 0.0 copy-start.1
  3.9 0.7 convert_element_type.14
  4.5 0.1 broadcast_multiply_fusion
  4.6 0.8 fusion.5
  5.4 1.7 fusion.4.ffn_row
  7.1 1.3 pad.23.out_row
  8.4 0.0 copy-done.1
  8.4 96.1 %shard_map.203 = (bf16[2,4,4,2,16,640]{5,4,3,2,1,0:T(8,128)(2,1)}, bf16[2,4,4,2,16,7296]{5,4,3,2,1,0:T(8,128)(2,1)}, bf16[1024,512]{1,0:T(8,128)(2,1)}, f32[1024...) custom-call(bf16[16,640]{1,0:T(8,128)(2,1)} %copy-done.1, ...), custom_call_target="tpu_custom_call" | custom-call | tf_op jit(solution)/shard_map/pallas_call | solution.py:653
  104.6 136.4 %shard_map.204 = (bf16[256,896]{1,0:T(8,128)(2,1)}, bf16[256,896]{1,0:T(8,128)(2,1)}, f32[16,1152]{1,0:T(8,128)}, f32[16,7296]{1,0:T(8,128)}) custom-call(bf16[2,4,4,2,16,640]{5,4,3,2,1,0:T(8,128)(2,1)} %get-tuple-element.28.attn_kept, bf16[1024,7296]{1,0:T(8,128)(2,1)} %bitcast.21, bf16[1024,512]{1,0:T(8,128)(2,1)} %get-tuple-element.30.w_out_kept, ...), custom_call_target="tpu_custom_call" | custom-call | tf_op jit(solution)/shard_map/pallas_call | solution.py:1011
  241.0 0.0 copy-start
  241.0 1.9 slice_bitcast_fusion
  242.9 0.8 slice_bitcast_fusion.1
  243.7 0.7 copy.29
  244.4 0.8 slice_bitcast_fusion.2
  245.1 0.6 copy.30
  245.8 1.3 constant_dynamic-slice_fusion.1
  247.0 1.3 constant_dynamic-slice_fusion
  248.3 1.5 slice_reduce_fusion
  249.8 1.8 copy.34
  251.6 0.0 copy-done
  251.6 0.8 copy.35
  (1 shorter events, 0.0 us)
Async XLA Ops:
  3.8 4.6 %copy-start.1 = (bf16[16,640]{1,0:T(8,128)(2,1)}, bf16[16,640]{1,0:T(8,128)(2,1)S(1)}, u32[]{:S(2)}) copy-start(bf16[16,640]{1,0:T(8,128)(2,1)S(1)} %dynamic_update_slice.3.attn_row) | copy-start | bytes 61444
  241.0 10.6 %copy-start = (bf16[256,896]{1,0:T(8,128)(2,1)S(1)}, bf16[256,896]{1,0:T(8,128)(2,1)}, u32[]{:S(2)}) copy-start(bf16[256,896]{1,0:T(8,128)(2,1)} %get-tuple-element.42) | copy-start | bytes 1376260
